TPU v7x, 32 devices: a whole 2x2x4 slice. The times are simulated.
32 devices in a mesh: seq: 4 (over y, x), shard: 8 (over z, core).
Axes of the slice: x: 2, y: 2, z: 4, core: 2. Of those that a mesh axis runs over, the one named last changes fastest.
Arguments:
- hidden_in: bfloat16 [16, 2048, 768], P('shard', 'seq'), may hold values from -6 to 6
- seq_lengths: int32 [16], P('shard'), may hold values from 1 to 2048, as said below
- w_qkv: bfloat16 [768, 2304], P('shard'), may hold values from -0.21875 to 0.21875
- b_query: bfloat16 [768], P('shard'), may hold values from -1.5 to 1.5
- b_value: bfloat16 [768], P('shard'), may hold values from -0.5 to 0.5
- w_out: bfloat16 [768, 768], P('shard'), may hold values from -6 to 6
- b_out: bfloat16 [768], P('shard'), may hold values from -1 to 1
- ln1_gain: bfloat16 [768], P('shard'), may hold values from 0.5 to 1.5
- ln1_bias: bfloat16 [768], P('shard'), may hold values from -1 to 1
- w_up: bfloat16 [768, 3072], P('shard'), may hold values from -0.21875 to 0.21875
- b_up: bfloat16 [3072], P('shard'), may hold values from -1 to 1
- w_down: bfloat16 [3072, 768], P('shard'), may hold values from -0.109375 to 0.109375
- b_down: bfloat16 [768], P('shard'), may hold values from -1 to 1
- ln2_gain: bfloat16 [768], P('shard'), may hold values from 0.5 to 1.5
- ln2_bias: bfloat16 [768], P('shard'), may hold values from -1 to 1
- cotangent: bfloat16 [16, 2048, 768], P('shard', 'seq'), may hold values from -6 to 6
Outputs:
- output: bfloat16 [16, 2048, 768], P('shard', 'seq')
- grad_input: bfloat16 [16, 2048, 768], P('shard', 'seq')
- grad_w_qkv: float32 [768, 2304], P('shard')
- grad_b_query: float32 [768], P('shard')
- grad_b_value: float32 [768], P('shard')
- grad_w_out: float32 [768, 768], P('shard')
- grad_b_out: float32 [768], P('shard')
- grad_ln1_gain: float32 [768], P('shard')
- grad_ln1_bias: float32 [768], P('shard')
- grad_w_up: float32 [768, 3072], P('shard')
- grad_b_up: float32 [3072], P('shard')
- grad_w_down: float32 [3072, 768], P('shard')
- grad_b_down: float32 [768], P('shard')
- grad_ln2_gain: float32 [768], P('shard')
- grad_ln2_bias: float32 [768], P('shard')
Inputs may be any that keep to these rules, and one draw needn't show every extreme that they name: `seq_lengths`: of sequences 2 i and 2 i + 1, at least one has all 2048 positions valid.
All inputs are finite; a program needn't handle non-finite values.
Results may differ from a plain program's by a relative error of at most 0.018.
Values may be sent and summed in bfloat16 or wider, within the bound.
A program may use at most 192 MiB of HBM per device.

v0:
```python
import jax
import jax.numpy as jnp
from jax import lax
from jax.sharding import PartitionSpec as P

DH = 64


EPS = 1e-12
NEG_FILL = -1e30
HALF_ROOT = 0.7071067811865476
INV_ROOT_TAU = 0.3989422804014327


def dot_rows(left_op, right_op):
    return lax.dot_general(
        left_op, right_op, (((0,), (0,)), ((), ())), preferred_element_type=jnp.float32
    )


def dot_last(left_op, right_op):
    return lax.dot_general(
        left_op, right_op, (((1,), (1,)), ((), ())), preferred_element_type=jnp.float32
    )


def owner_order(grad_arr, shard_count, group_count):
    rows = grad_arr.shape[0]
    piece = rows // (shard_count * group_count)
    rest = grad_arr.shape[1:]
    split = grad_arr.reshape((shard_count, group_count, piece) + rest)
    return jnp.swapaxes(split, 0, 1).reshape(grad_arr.shape)


def reorder_all(grad_list, shard_count, group_count):
    return tuple((owner_order(grad_arr, shard_count, group_count) for grad_arr in grad_list))


def norm_forward(hidden, gain_vec, shift_vec):
    mean_val = jnp.mean(hidden, axis=-1, keepdims=True)
    centered = hidden - mean_val
    inv_std = lax.rsqrt(jnp.mean(centered * centered, axis=-1, keepdims=True) + EPS)
    normed = centered * inv_std
    return (normed * gain_vec + shift_vec, normed, inv_std)


def norm_backward(grad_out, normed, inv_std, gain_vec):
    grad_gain = jnp.sum(grad_out * normed, axis=0)
    grad_shift = jnp.sum(grad_out, axis=0)
    scaled = grad_out * gain_vec
    grad_in = inv_std * (
        scaled
        - jnp.mean(scaled, axis=-1, keepdims=True)
        - normed * jnp.mean(scaled * normed, axis=-1, keepdims=True)
    )
    return (grad_in, grad_gain, grad_shift)


def gelu_parts(pre_act):
    cdf_val = 0.5 * (1.0 + lax.erf(pre_act * HALF_ROOT))
    pdf_val = jnp.exp(-0.5 * pre_act * pre_act) * INV_ROOT_TAU
    return (pre_act * cdf_val, cdf_val + pre_act * pdf_val)


def masked_scores(query_blk, keys_all, key_valid, scale_val):
    scores = (
        jnp.einsum("bhd,khd->hbk", query_blk, keys_all, preferred_element_type=jnp.float32)
        * scale_val
    )
    return jnp.where(key_valid[None, None, :], scores, NEG_FILL)


def attend_forward(head_data, length, block_rows):
    seq_len = head_data.shape[0]
    heads_here = head_data.shape[2]
    head_size = head_data.shape[3]
    keys_all = head_data[:, 1]
    values_all = head_data[:, 2]
    key_valid = jnp.arange(seq_len) < length
    scale_val = head_size ** (-0.5)
    query_blocks = head_data[:, 0].reshape(seq_len // block_rows, block_rows, heads_here, head_size)

    def one_block(query_blk):
        scores = masked_scores(query_blk, keys_all, key_valid, scale_val)
        row_max = jnp.max(scores, axis=-1, keepdims=True)
        exp_scores = jnp.exp(scores - row_max)
        row_sum = jnp.sum(exp_scores, axis=-1, keepdims=True)
        attn_prob = (exp_scores / row_sum).astype(jnp.bfloat16)
        out_blk = jnp.einsum(
            "hbk,khd->bhd", attn_prob, values_all, preferred_element_type=jnp.float32
        )
        return (out_blk, (row_max + jnp.log(row_sum))[..., 0])

    out_blocks, row_lse = lax.map(one_block, query_blocks)
    return (out_blocks.reshape(seq_len, heads_here, head_size), row_lse)


def attend_backward(head_data, grad_att, row_lse, length, block_rows):
    seq_len = head_data.shape[0]
    heads_here = head_data.shape[2]
    head_size = head_data.shape[3]
    keys_all = head_data[:, 1]
    values_all = head_data[:, 2]
    key_valid = jnp.arange(seq_len) < length
    scale_val = head_size ** (-0.5)
    block_count = seq_len // block_rows
    query_blocks = head_data[:, 0].reshape(block_count, block_rows, heads_here, head_size)
    grad_blocks = grad_att.reshape(block_count, block_rows, heads_here, head_size)

    def one_block(carried, pieces):
        grad_keys, grad_values = carried
        query_blk, grad_blk, lse_blk = pieces
        scores = masked_scores(query_blk, keys_all, key_valid, scale_val)
        attn_prob = jnp.exp(scores - lse_blk[..., None])
        grad_prob = jnp.einsum(
            "bhd,khd->hbk", grad_blk, values_all, preferred_element_type=jnp.float32
        )
        row_dot = jnp.sum(grad_prob * attn_prob, axis=-1, keepdims=True)
        grad_scores = (attn_prob * (grad_prob - row_dot)).astype(jnp.bfloat16)
        grad_query = (
            jnp.einsum("hbk,khd->bhd", grad_scores, keys_all, preferred_element_type=jnp.float32)
            * scale_val
        )
        grad_keys = (
            grad_keys
            + jnp.einsum("hbk,bhd->khd", grad_scores, query_blk, preferred_element_type=jnp.float32)
            * scale_val
        )
        grad_values = grad_values + jnp.einsum(
            "hbk,bhd->khd",
            attn_prob.astype(jnp.bfloat16),
            grad_blk,
            preferred_element_type=jnp.float32,
        )
        return ((grad_keys, grad_values), grad_query)

    zeros_kv = jnp.zeros((seq_len, heads_here, head_size), jnp.float32)
    (grad_keys, grad_values), grad_queries = lax.scan(
        one_block, (zeros_kv, zeros_kv), (query_blocks, grad_blocks, row_lse)
    )
    grad_queries = grad_queries.reshape(seq_len, heads_here, head_size)
    return jnp.stack([grad_queries, grad_keys, grad_values], axis=1).astype(jnp.bfloat16)


def per_device(
    hidden_in,
    seq_lengths,
    w_qkv,
    b_query,
    b_value,
    w_out,
    b_out,
    ln1_gain,
    ln1_bias,
    w_up,
    b_up,
    w_down,
    b_down,
    ln2_gain,
    ln2_bias,
    cotangent,
):
    group_count = lax.axis_size("seq")
    shard_count = lax.axis_size("shard")
    seq_count = hidden_in.shape[0]
    pos_count = hidden_in.shape[1]
    model_width = hidden_in.shape[2]
    tok_count = seq_count * pos_count
    full_len = pos_count * group_count
    group_width = model_width // group_count
    heads_here = group_width // DH
    block_rows = min(512, full_len)
    gathered = (
        lax.all_gather(w_qkv, "shard", axis=0, tiled=True),
        lax.all_gather(b_query, "shard", axis=0, tiled=True),
        lax.all_gather(b_value, "shard", axis=0, tiled=True),
        lax.all_gather(w_out, "shard", axis=0, tiled=True),
        lax.all_gather(b_out, "shard", axis=0, tiled=True),
        lax.all_gather(ln1_gain, "shard", axis=0, tiled=True),
        lax.all_gather(ln1_bias, "shard", axis=0, tiled=True),
        lax.all_gather(w_up, "shard", axis=0, tiled=True),
        lax.all_gather(b_up, "shard", axis=0, tiled=True),
        lax.all_gather(w_down, "shard", axis=0, tiled=True),
        lax.all_gather(b_down, "shard", axis=0, tiled=True),
        lax.all_gather(ln2_gain, "shard", axis=0, tiled=True),
        lax.all_gather(ln2_bias, "shard", axis=0, tiled=True),
    )
    (
        qkv_weight,
        query_bias,
        value_bias,
        out_weight,
        out_bias,
        gain_one,
        shift_one,
        up_weight,
        up_bias,
        down_weight,
        down_bias,
        gain_two,
        shift_two,
    ) = gathered
    gain_one = gain_one.astype(jnp.float32)
    gain_two = gain_two.astype(jnp.float32)
    tokens = hidden_in.reshape(tok_count, model_width)
    qkv_bias = jnp.concatenate([query_bias, jnp.zeros_like(query_bias), value_bias]).astype(
        jnp.float32
    )
    qkv_tok = (jnp.dot(tokens, qkv_weight, preferred_element_type=jnp.float32) + qkv_bias).astype(
        jnp.bfloat16
    )
    head_data = lax.all_to_all(
        qkv_tok.reshape(seq_count, pos_count, 3, group_count, group_width),
        "seq",
        split_axis=3,
        concat_axis=1,
        tiled=True,
    )
    head_data = head_data.reshape(seq_count, full_len, 3, heads_here, DH)
    attended_list = []
    lse_list = []
    for seq_pos in range(seq_count):
        out_seq, lse_seq = attend_forward(head_data[seq_pos], seq_lengths[seq_pos], block_rows)
        attended_list.append(out_seq)
        lse_list.append(lse_seq)
    attended_heads = (
        jnp.stack(attended_list).astype(jnp.bfloat16).reshape(seq_count, full_len, 1, group_width)
    )
    attended = lax.all_to_all(
        attended_heads, "seq", split_axis=1, concat_axis=2, tiled=True
    ).reshape(tok_count, model_width)
    projected = jnp.dot(attended, out_weight, preferred_element_type=jnp.float32) + out_bias.astype(
        jnp.float32
    )
    ln_one, normed_one, inv_one = norm_forward(
        tokens.astype(jnp.float32) + projected, gain_one, shift_one.astype(jnp.float32)
    )
    ln_low = ln_one.astype(jnp.bfloat16)
    pre_act = jnp.dot(ln_low, up_weight, preferred_element_type=jnp.float32) + up_bias.astype(
        jnp.float32
    )
    act_val, act_slope = gelu_parts(pre_act)
    act_low = act_val.astype(jnp.bfloat16)
    ffn_out = jnp.dot(act_low, down_weight, preferred_element_type=jnp.float32) + down_bias.astype(
        jnp.float32
    )
    result, normed_two, inv_two = norm_forward(
        ln_one + ffn_out, gain_two, shift_two.astype(jnp.float32)
    )
    output = result.astype(jnp.bfloat16).reshape(seq_count, pos_count, model_width)
    grad_y = cotangent.reshape(tok_count, model_width).astype(jnp.float32)
    grad_two, grad_gain_two, grad_shift_two = norm_backward(grad_y, normed_two, inv_two, gain_two)
    grad_ffn = grad_two.astype(jnp.bfloat16)
    grad_down_bias = jnp.sum(grad_ffn, axis=0, dtype=jnp.float32)
    grad_down_weight = dot_rows(act_low, grad_ffn)
    grad_pre = (dot_last(grad_ffn, down_weight) * act_slope).astype(jnp.bfloat16)
    grad_up_bias = jnp.sum(grad_pre, axis=0, dtype=jnp.float32)
    grad_up_weight = dot_rows(ln_low, grad_pre)
    grad_ln = dot_last(grad_pre, up_weight) + grad_two
    grad_one, grad_gain_one, grad_shift_one = norm_backward(grad_ln, normed_one, inv_one, gain_one)
    grad_proj = grad_one.astype(jnp.bfloat16)
    grad_out_bias = jnp.sum(grad_proj, axis=0, dtype=jnp.float32)
    grad_out_weight = dot_rows(attended, grad_proj)
    grad_att = dot_last(grad_proj, out_weight).astype(jnp.bfloat16)
    grad_heads = lax.all_to_all(
        grad_att.reshape(seq_count, pos_count, group_count, group_width),
        "seq",
        split_axis=2,
        concat_axis=1,
        tiled=True,
    )
    grad_heads = grad_heads.reshape(seq_count, full_len, heads_here, DH)
    grad_list = []
    for seq_pos in range(seq_count):
        grad_list.append(
            attend_backward(
                head_data[seq_pos],
                grad_heads[seq_pos],
                lse_list[seq_pos],
                seq_lengths[seq_pos],
                block_rows,
            )
        )
    grad_qkv_heads = jnp.stack(grad_list).reshape(seq_count, full_len, 3, 1, group_width)
    grad_qkv = lax.all_to_all(
        grad_qkv_heads, "seq", split_axis=1, concat_axis=3, tiled=True
    ).reshape(tok_count, 3 * model_width)
    grad_qkv_weight = dot_rows(tokens, grad_qkv)
    grad_query_bias = jnp.sum(grad_qkv[:, :model_width], axis=0, dtype=jnp.float32)
    grad_value_bias = jnp.sum(grad_qkv[:, 2 * model_width :], axis=0, dtype=jnp.float32)
    grad_input = (
        (dot_last(grad_qkv, qkv_weight) + grad_one)
        .astype(jnp.bfloat16)
        .reshape(seq_count, pos_count, model_width)
    )
    attn_list = (
        grad_qkv_weight,
        grad_query_bias,
        grad_value_bias,
        grad_out_weight,
        grad_out_bias,
        grad_gain_one,
        grad_shift_one,
    )
    every_grad = attn_list + (
        grad_up_weight,
        grad_up_bias,
        grad_down_weight,
        grad_down_bias,
        grad_gain_two,
        grad_shift_two,
    )
    every_grad = reorder_all(every_grad, shard_count, group_count)
    shares = (
        lax.psum_scatter(every_grad[0], ("seq", "shard"), scatter_dimension=0, tiled=True),
        lax.psum_scatter(every_grad[1], ("seq", "shard"), scatter_dimension=0, tiled=True),
        lax.psum_scatter(every_grad[2], ("seq", "shard"), scatter_dimension=0, tiled=True),
        lax.psum_scatter(every_grad[3], ("seq", "shard"), scatter_dimension=0, tiled=True),
        lax.psum_scatter(every_grad[4], ("seq", "shard"), scatter_dimension=0, tiled=True),
        lax.psum_scatter(every_grad[5], ("seq", "shard"), scatter_dimension=0, tiled=True),
        lax.psum_scatter(every_grad[6], ("seq", "shard"), scatter_dimension=0, tiled=True),
        lax.psum_scatter(every_grad[7], ("seq", "shard"), scatter_dimension=0, tiled=True),
        lax.psum_scatter(every_grad[8], ("seq", "shard"), scatter_dimension=0, tiled=True),
        lax.psum_scatter(every_grad[9], ("seq", "shard"), scatter_dimension=0, tiled=True),
        lax.psum_scatter(every_grad[10], ("seq", "shard"), scatter_dimension=0, tiled=True),
        lax.psum_scatter(every_grad[11], ("seq", "shard"), scatter_dimension=0, tiled=True),
        lax.psum_scatter(every_grad[12], ("seq", "shard"), scatter_dimension=0, tiled=True),
    )
    (
        share_qkv,
        share_qbias,
        share_vbias,
        share_outw,
        share_outb,
        share_gain_one,
        share_shift_one,
        share_upw,
        share_upb,
        share_downw,
        share_downb,
        share_gain_two,
        share_shift_two,
    ) = shares
    summed = (
        lax.all_gather(share_qkv.astype(jnp.bfloat16), "seq", axis=0, tiled=True).astype(
            share_qkv.dtype
        ),
        lax.all_gather(share_qbias.astype(jnp.bfloat16), "seq", axis=0, tiled=True).astype(
            share_qbias.dtype
        ),
        lax.all_gather(share_vbias.astype(jnp.bfloat16), "seq", axis=0, tiled=True).astype(
            share_vbias.dtype
        ),
        lax.all_gather(share_outw.astype(jnp.bfloat16), "seq", axis=0, tiled=True).astype(
            share_outw.dtype
        ),
        lax.all_gather(share_outb.astype(jnp.bfloat16), "seq", axis=0, tiled=True).astype(
            share_outb.dtype
        ),
        lax.all_gather(share_gain_one.astype(jnp.bfloat16), "seq", axis=0, tiled=True).astype(
            share_gain_one.dtype
        ),
        lax.all_gather(share_shift_one.astype(jnp.bfloat16), "seq", axis=0, tiled=True).astype(
            share_shift_one.dtype
        ),
        lax.all_gather(share_upw.astype(jnp.bfloat16), "seq", axis=0, tiled=True).astype(
            share_upw.dtype
        ),
        lax.all_gather(share_upb.astype(jnp.bfloat16), "seq", axis=0, tiled=True).astype(
            share_upb.dtype
        ),
        lax.all_gather(share_downw.astype(jnp.bfloat16), "seq", axis=0, tiled=True).astype(
            share_downw.dtype
        ),
        lax.all_gather(share_downb.astype(jnp.bfloat16), "seq", axis=0, tiled=True).astype(
            share_downb.dtype
        ),
        lax.all_gather(share_gain_two.astype(jnp.bfloat16), "seq", axis=0, tiled=True).astype(
            share_gain_two.dtype
        ),
        lax.all_gather(share_shift_two.astype(jnp.bfloat16), "seq", axis=0, tiled=True).astype(
            share_shift_two.dtype
        ),
    )
    return (
        output,
        grad_input,
        summed[0],
        summed[1],
        summed[2],
        summed[3],
        summed[4],
        summed[5],
        summed[6],
        summed[7],
        summed[8],
        summed[9],
        summed[10],
        summed[11],
        summed[12],
    )


def solution(mesh):
    in_specs = (
        P("shard", "seq", None),
        P("shard"),
        P("shard", None),
        P("shard"),
        P("shard"),
        P("shard", None),
        P("shard"),
        P("shard"),
        P("shard"),
        P("shard", None),
        P("shard"),
        P("shard", None),
        P("shard"),
        P("shard"),
        P("shard"),
        P("shard", "seq", None),
    )
    out_specs = (
        P("shard", "seq", None),
        P("shard", "seq", None),
        P("shard", None),
        P("shard"),
        P("shard"),
        P("shard", None),
        P("shard"),
        P("shard"),
        P("shard"),
        P("shard", None),
        P("shard"),
        P("shard", None),
        P("shard"),
        P("shard"),
        P("shard"),
    )
    return jax.shard_map(
        per_device, mesh=mesh, in_specs=in_specs, out_specs=out_specs, check_vma=False
    )
```

profile of v0, /device:TPU:0, one launch (start us, length us, event | category | flops | bytes accessed | tf_op | source)
XLA Modules:
  0.0 979.8 jit_solution(11414818758463418126)
XLA Ops:
  18.0 32.2 %all-reduce.27 = (bf16[768]{0:T(1024)(128)(2,1)S(1)}, bf16[768]{0:T(1024)(128)(2,1)S(1)}, bf16[768]{0:T(1024)(128)(2,1)}, bf16[768]{0:T(1024)(128)(2,1)}, bf16[7...) all-reduce(bf16[768]{0:T(1024)(128)(2,1)S(1)} %dynamic-update-slice, ...), channel_id=1, replica_groups=mesh['seq'=4,'shard'=8] {'shard'}, use_global_device_ids=true, to_apply=%add.1 | all-reduce | flops 6144 | bytes 24576
  54.5 8.5 add_convert_fusion
  63.1 12.8 %reshape.544 = bf16[2,512,3,4,192]{4,3,2,1,0:T(4,128)(2,1)} reshape(bf16[1024,2304]{1,0:T(8,128)(2,1)} %add_convert_fusion) | data formatting | bytes 9437184 | tf_op jit(solution)/shard_map/reshape | solution.py:213
  75.9 17.4 %copy.144 = bf16[2,512,3,4,192]{1,0,4,2,3:T(2,128)(2,1)} copy(bf16[2,512,3,4,192]{4,3,2,1,0:T(4,128)(2,1)} %reshape.544) | data formatting | bytes 9437184 | tf_op jit(solution)/shard_map/reshape | solution.py:213
  99.6 52.5 %all-to-all-done = bf16[2,512,3,4,192]{1,0,4,2,3:T(2,128)(2,1)} async-done(((bf16[2,512,3,4,192]{1,0,4,2,3:T(2,128)(2,1)}), bf16[2,512,3,4,192]{1,0,4,2,3:T(2,128)(2,1)}, u32[]{:S(2)}, u32[]{:S(2)}) %all-to-all-start) | async-done | bytes 4718624 | tf_op jit(solution)/shard_map/all_to_all | solution.py:212
  152.1 10.6 %fusion.115 = (bf16[1,4,512,3,1,192]{2,0,5,3,1,4:T(2,128)(2,1)S(1)}, bf16[1,4,512,3,1,192]{2,0,5,3,1,4:T(2,128)(2,1)}) fusion(bf16[2,4,512,3,1,192]{2,0,5,3,1,4:T(2,128)(2,1)} %bitcast.3), kind=kLoop, calls=%fused_computation.175 | loop fusion | bytes 9437184 | tf_op jit(solution)/shard_map/slice | solution.py:223
  171.3 37.2 %while.56 = (s32[]{:T(128)}, bf16[4,512,3,64]{1,3,2,0:T(8,128)(2,1)S(1)}, f32[4,3,512]{2,1,0:T(4,128)S(1)}, bf16[4,512,3,64]{1,3,2,0:T(8,128)(2,1)S(1)}, bf16[20...) while((s32[]{:T(128)}, ...), condition=%wide.region_3.4_spmd.clone, body=%wide.region_0.3_spmd.clone.sunk | while | flops 843055616 | bytes 39979108 | solution.py:94
  208.5 7.7 copy.148
  216.2 5.9 squeeze.61
  227.6 39.2 %while.57 = (s32[]{:T(128)}, bf16[4,512,3,64]{1,3,2,0:T(8,128)(2,1)}, f32[4,3,512]{2,1,0:T(4,128)S(1)}, bf16[4,512,3,64]{1,3,2,0:T(8,128)(2,1)S(1)}, bf16[2048,3...) while((s32[]{:T(128)}, ...), condition=%wide.region_7.8_spmd.clone, body=%wide.region_4.7_spmd.clone.sunk | while | flops 843055616 | bytes 39975520 | solution.py:94
  277.1 6.1 copy.151
  287.9 12.7 %all-gather = bf16[8,1,384]{2,1,0:T(2,128)(2,1)S(1)} all-gather(bf16[1,1,384]{2,1,0:T(2,128)(2,1)S(1)} %reshape.506), channel_id=1, replica_groups=mesh['seq'=4,'shard'=8] {'shard'}, dimensions={0}, use_global_device_ids=true | all-gather | bytes 6912 | tf_op jit(solution)/shard_map/all_gather | solution.py:182
  302.0 10.6 %all-to-all-done.1 = bf16[2,2048,1,192]{3,0,2,1:T(2,128)(2,1)} async-done(((bf16[2,2048,1,192]{3,0,2,1:T(2,128)(2,1)}), bf16[2,2048,1,192]{3,0,2,1:T(2,128)(2,1)}, u32[]{:S(2)}, u32[]{:S(2)}) %all-to-all-start.1) | async-done | bytes 1572896 | tf_op jit(solution)/shard_map/all_to_all | solution.py:229
  312.5 5.8 copy.178
  325.9 12.1 %multiply_convert_fusion.2 = (bf16[1024,3072]{1,0:T(8,128)(2,1)}, f32[1024,3072]{1,0:T(8,128)}) fusion(f32[3072]{0:T(1024)S(1)} %bitcast.340, bf16[768,3072]{1,0:T(8,128)(2,1)} %all-gather.10.cloned.1.call-done, f32[1024,768]{1,0:T(8,128)S(1)} %get-tuple-element.615, f32[768]{0:T(1024)S(1)} %convert_element_type.210, f32[768]{0:T(1024)S(1)} %convert_element_type.209, ...), kind=kOutput, calls=%fused_computation.108 | convolution fusion | flops 4854644736 | bytes 26765312 | tf_op jit(solution)/shard_map/dot_general | solution.py:239
  338.1 8.8 fusion.119
  353.0 14.1 %convert_reduce_fusion = (f32[3072]{0:T(1024)}, bf16[1024,3072]{1,0:T(8,128)(2,1)S(1)}) fusion(f32[1024,3072]{1,0:T(8,128)} %get-tuple-element.617, f32[3072]{0:T(1024)S(1)} %bitcast.341, bf16[3072,768]{1,0:T(8,128)(2,1)S(1)} %copy-done.47, f32[1024,768]{1,0:T(8,128)S(1)} %get-tuple-element.590), kind=kOutput, calls=%fused_computation.107 | convolution fusion | flops 4873516032 | bytes 26763264 | tf_op jit(solution)/shard_map/dot_general | solution.py:22
  367.1 6.5 multiply_reduce_fusion.2
  378.8 7.9 fusion.110
  404.5 8.6 fusion.107
  428.2 130.5 %while.58 = (s32[]{:T(128)}, f32[2048,3,64]{0,2,1:T(8,128)}, f32[2048,3,64]{0,2,1:T(8,128)}, bf16[4,512,3,64]{1,3,2,0:T(8,128)(2,1)}, bf16[4,512,3,64]{1,3,2,0:T...) while((s32[]{:T(128)}, f32[2048,3,64]{0,2,1:T(8,128)}, ...), condition=%wide.region_18.19_spmd.clone, body=%wide.region_16.18_spmd.clone.sunk | while | flops 2062516736 | bytes 204919504 | solution.py:138
  432.5 5.8 multiply_reduce_fusion.9
  448.9 6.2 fusion.211
  474.9 5.8 fusion.209
  480.7 6.2 fusion.211
  496.7 5.9 multiply_reduce_fusion.9
  507.5 6.2 fusion.209
  513.7 6.6 fusion.211
  540.9 5.9 fusion.209
  546.8 6.4 fusion.211
  562.2 122.3 %while.59 = (s32[]{:T(128)}, f32[2048,3,64]{0,2,1:T(8,128)S(1)}, f32[2048,3,64]{0,2,1:T(8,128)}, bf16[4,512,3,64]{1,3,2,0:T(8,128)(2,1)}, bf16[4,512,3,64]{1,3,2...) while((s32[]{:T(128)}, f32[2048,3,64]{0,2,1:T(8,128)S(1)}, ...), condition=%wide.region_21.22_spmd.clone, body=%wide.region_19.21_spmd.clone.sunk | while | flops 2062516736 | bytes 214356272 | solution.py:138
  616.9 5.8 fusion.223
  641.7 6.0 fusion.224
  647.7 5.9 fusion.223
  672.2 6.4 fusion.224
  678.6 5.8 fusion.223
  701.9 16.1 %copy.159 = bf16[2,2048,3,1,192]{4,0,3,2,1:T(2,128)(2,1)} copy(bf16[2,2048,3,1,192]{1,4,3,2,0:T(8,128)(2,1)} %maximum_maximum_fusion) | data formatting | bytes 9437184 | tf_op jit(solution)/shard_map/stack | solution.py:284
  718.0 81.2 %all_to_all.60 = bf16[2,2048,3,1,192]{4,0,3,2,1:T(2,128)(2,1)} all-to-all(bf16[2,2048,3,1,192]{4,0,3,2,1:T(2,128)(2,1)} %copy.159), channel_id=1, replica_groups=mesh['seq'=4,'shard'=8] {'seq'}, dimensions={1} | all-to-all | bytes 9437184 | tf_op jit(solution)/shard_map/all_to_all | solution.py:285
  799.2 16.9 %copy.179 = bf16[2,4,512,3,1,192]{2,1,5,3,0,4:T(4,128)(2,1)} copy(bf16[2,4,512,3,1,192]{5,0,3,2,1,4:T(2,128)(2,1)} %bitcast.309) | data formatting | bytes 9437184 | tf_op jit(solution)/shard_map/all_to_all | solution.py:285
  816.1 9.4 copy.161
  842.0 9.0 all_gather.94
  854.6 40.1 %all-reduce.26 = (bf16[768]{0:T(1024)(128)(2,1)S(1)}, bf16[768]{0:T(1024)(128)(2,1)S(1)}, bf16[768]{0:T(1024)(128)(2,1)S(1)}, bf16[768]{0:T(1024)(128)(2,1)S(1)}...) all-reduce(f32[768]{0:T(1024)S(1)} %reshape.432, ...), channel_id=3, replica_groups=mesh['seq'=4,'shard'=8] {'seq','shard'}, use_global_device_ids=true, to_apply=%region_24.25.clone | all-reduce | flops 9216 | bytes 55296
  897.4 9.9 %all-reduce.28 = (bf16[96]{0:T(256)(128)(2,1)S(1)}, bf16[96]{0:T(256)(128)(2,1)S(1)}, bf16[96]{0:T(256)(128)(2,1)S(1)}, bf16[96]{0:T(256)(128)(2,1)S(1)}, bf16[9...) all-reduce(bf16[96]{0:T(256)(128)(2,1)S(1)} %dynamic-update-slice.8, ...), channel_id=1, replica_groups=mesh['seq'=4,'shard'=8] {'seq'}, use_global_device_ids=true, to_apply=%add.8 | all-reduce | flops 1152 | bytes 4608
  911.9 8.5 add_convert_fusion.1
  921.4 12.6 %all_gather.98 = bf16[96,3072]{1,0:T(8,128)(2,1)S(1)} all-gather(bf16[24,3072]{1,0:T(8,128)(2,1)S(1)} %convert_element_type.243), channel_id=1, replica_groups=mesh['seq'=4,'shard'=8] {'seq'}, dimensions={0}, use_global_device_ids=true | all-gather | bytes 737280 | tf_op jit(solution)/shard_map/all_gather | solution.py:366
  936.2 10.3 %all_gather.100 = bf16[384,768]{1,0:T(8,128)(2,1)S(1)} all-gather(bf16[96,768]{1,0:T(8,128)(2,1)S(1)} %convert_element_type.248), channel_id=1, replica_groups=mesh['seq'=4,'shard'=8] {'seq'}, dimensions={0}, use_global_device_ids=true | all-gather | bytes 737280 | tf_op jit(solution)/shard_map/all_gather | solution.py:372
  947.6 12.9 %reduce-scatter.5.cloned.1.call-done = f32[24,2304]{1,0:T(8,128)} async-done(((f32[768,2304]{1,0:T(8,128)}), f32[24,2304]{1,0:T(8,128)}) %reduce-scatter.5.cloned.1.call-update) | async-done | bytes 221200 | tf_op jit(solution)/shard_map/reduce_scatter | solution.py:315
  961.5 10.3 %all_gather.91 = bf16[96,2304]{1,0:T(8,128)(2,1)S(1)} all-gather(bf16[24,2304]{1,0:T(8,128)(2,1)S(1)} %convert_element_type.226), channel_id=1, replica_groups=mesh['seq'=4,'shard'=8] {'seq'}, dimensions={0}, use_global_device_ids=true | all-gather | bytes 552960 | tf_op jit(solution)/shard_map/all_gather | solution.py:345
  (427 shorter events, 398.1 us)
Async XLA Ops:
  7.2 47.3 %all-gather.6.cloned.1.call-start = ((), (), s32[]{:S(2)}) async-start(), calls=%async_computation.8 | async-start | bytes 3981312 | tf_op jit(solution)/shard_map/all_gather | solution.py:174
  7.9 313.6 %all-gather.8.cloned.1.call-start = ((), (), s32[]{:S(2)}) async-start(), calls=%async_computation.9 | async-start | bytes 1327104 | tf_op jit(solution)/shard_map/all_gather | solution.py:177
  8.7 317.3 %all-gather.10.cloned.1.call-start = ((), (), s32[]{:S(2)}) async-start(), calls=%async_computation.10 | async-start | bytes 5308416 | tf_op jit(solution)/shard_map/all_gather | solution.py:181
  93.3 58.8 %all-to-all-start = ((bf16[2,512,3,4,192]{1,0,4,2,3:T(2,128)(2,1)}), bf16[2,512,3,4,192]{1,0,4,2,3:T(2,128)(2,1)}, u32[]{:S(2)}, u32[]{:S(2)}) async-start(bf16[2,512,3,4,192]{1,0,4,2,3:T(2,128)(2,1)} %copy.144), calls=%async_computation | async-start | bytes 9437184 | tf_op jit(solution)/shard_map/all_to_all | solution.py:212
  98.4 239.7 %all-gather.12.cloned.1.call-start = ((), (), s32[]{:S(2)}) async-start(), calls=%async_computation.11 | async-start | bytes 5308416 | tf_op jit(solution)/shard_map/all_gather | solution.py:183
  208.5 7.7 copy-start.6
  208.5 7.7 copy-start.12
  208.5 7.7 copy-start.14
  208.5 7.7 copy-start.30
  266.7 10.3 %copy-start.4 = (bf16[2048,3,64]{0,2,1:T(8,128)(2,1)}, bf16[2048,3,64]{0,2,1:T(8,128)(2,1)S(1)}, u32[]{:S(2)}) copy-start(bf16[2048,3,64]{0,2,1:T(8,128)(2,1)S(1)} %get-tuple-element.977) | copy-start | bytes 2359300
  266.7 10.3 %copy-start.10 = (bf16[2048,3,64]{0,2,1:T(8,128)(2,1)}, bf16[2048,3,64]{0,2,1:T(8,128)(2,1)S(1)}, u32[]{:S(2)}) copy-start(bf16[2048,3,64]{0,2,1:T(8,128)(2,1)S(1)} %get-tuple-element.979) | copy-start | bytes 2359300
  266.7 10.3 %copy-start.13 = (bf16[4,512,3,64]{1,3,2,0:T(8,128)(2,1)}, bf16[4,512,3,64]{1,3,2,0:T(8,128)(2,1)S(1)}, u32[]{:S(2)}) copy-start(bf16[4,512,3,64]{1,3,2,0:T(8,128)(2,1)S(1)} %get-tuple-element.989) | copy-start | bytes 2359300
  266.7 10.3 %copy-start.31 = (f32[4,3,512]{2,1,0:T(4,128)}, f32[4,3,512]{2,1,0:T(4,128)S(1)}, u32[]{:S(2)}) copy-start(f32[4,3,512]{2,1,0:T(4,128)S(1)} %get-tuple-element.903) | copy-start | bytes 73732
  277.1 10.8 %copy-start.44 = (bf16[768]{0:T(1024)(128)(2,1)S(1)}, bf16[768]{0:T(1024)(128)(2,1)}, u32[]{:S(2)}) copy-start(bf16[768]{0:T(1024)(128)(2,1)} %get-tuple-element.574) | copy-start | bytes 4612
  277.1 10.8 %copy-start.43 = (bf16[768]{0:T(1024)(128)(2,1)S(1)}, bf16[768]{0:T(1024)(128)(2,1)}, u32[]{:S(2)}) copy-start(bf16[768]{0:T(1024)(128)(2,1)} %get-tuple-element.576) | copy-start | bytes 4612
  277.1 10.8 %copy-start.42 = (bf16[768]{0:T(1024)(128)(2,1)S(1)}, bf16[768]{0:T(1024)(128)(2,1)}, u32[]{:S(2)}) copy-start(bf16[768]{0:T(1024)(128)(2,1)} %get-tuple-element.575) | copy-start | bytes 4612
  277.1 10.8 %copy-start.46 = (bf16[384]{0:T(512)(128)(2,1)S(1)}, bf16[384]{0:T(512)(128)(2,1)}, u32[]{:S(2)}) copy-start(bf16[384]{0:T(512)(128)(2,1)} %param.34) | copy-start | bytes 2308
  277.1 23.5 %copy-start.41 = (bf16[768]{0:T(1024)(128)(2,1)S(1)}, bf16[768]{0:T(1024)(128)(2,1)}, u32[]{:S(2)}) copy-start(bf16[768]{0:T(1024)(128)(2,1)} %get-tuple-element.577) | copy-start | bytes 4612
  277.1 23.5 %copy-start.40 = (bf16[768]{0:T(1024)(128)(2,1)S(1)}, bf16[768]{0:T(1024)(128)(2,1)}, u32[]{:S(2)}) copy-start(bf16[768]{0:T(1024)(128)(2,1)} %get-tuple-element.579) | copy-start | bytes 4612
  283.2 17.5 %copy-start.15 = (bf16[2,512,768]{2,1,0:T(8,128)(2,1)S(1)}, bf16[2,512,768]{2,1,0:T(8,128)(2,1)}, u32[]{:S(2)}) copy-start(bf16[2,512,768]{2,1,0:T(8,128)(2,1)} %param.39) | copy-start | bytes 4718596
  283.2 18.8 %copy-start.39 = (bf16[768]{0:T(1024)(128)(2,1)S(1)}, bf16[768]{0:T(1024)(128)(2,1)}, u32[]{:S(2)}) copy-start(bf16[768]{0:T(1024)(128)(2,1)} %get-tuple-element.578) | copy-start | bytes 4612
  283.2 29.3 %all-to-all-start.1 = ((bf16[2,2048,1,192]{3,0,2,1:T(2,128)(2,1)}), bf16[2,2048,1,192]{3,0,2,1:T(2,128)(2,1)}, u32[]{:S(2)}, u32[]{:S(2)}) async-start(bf16[2,2048,1,192]{3,0,2,1:T(2,128)(2,1)} %copy.151), calls=%async_computation.1 | async-start | bytes 4194304 | tf_op jit(solution)/shard_map/all_to_all | solution.py:229
  287.8 553.3 %reduce-scatter.7.cloned.1.call-start = ((), (), s32[]{:S(2)}) async-start(), calls=%async_computation.13 | async-start | bytes 2433024 | tf_op jit(solution)/shard_map/reduce_scatter | solution.py:318
  350.1 17.0 %slice-start = ((s8[4718592]{0:T(1024)(128)(4,1)}), s8[4194304]{0:T(1024)(128)(4,1)S(1)}, s32[]{:S(2)}) async-start(s8[4718592]{0:T(1024)(128)(4,1)} %bitcast.342), calls=%async_computation.16 | async-start | bytes 8388608
  353.0 14.1 %copy-start.19 = (f32[1024,768]{1,0:T(8,128)}, f32[1024,768]{1,0:T(8,128)S(1)}, u32[]{:S(2)}) copy-start(f32[1024,768]{1,0:T(8,128)S(1)} %get-tuple-element.590) | copy-start | bytes 9437188
  353.0 14.1 %slice-start.1 = ((s8[4718592]{0:T(1024)(128)(4,1)}), s8[524288]{0:T(1024)(128)(4,1)S(1)}, s32[]{:S(2)}) async-start(s8[4718592]{0:T(1024)(128)(4,1)} %bitcast.342), calls=%async_computation.17 | async-start | bytes 1048576
  378.8 541.7 %reduce-scatter.9.cloned.1.call-start = ((), (), s32[]{:S(2)}) async-start(), calls=%async_computation.14 | async-start | bytes 9732096 | tf_op jit(solution)/shard_map/reduce_scatter | solution.py:322
  400.8 22.2 %all-to-all-start.2 = ((bf16[2,512,4,192]{1,0,3,2:T(2,128)(2,1)}), bf16[2,512,4,192]{1,0,3,2:T(2,128)(2,1)S(1)}, u32[]{:S(2)}, u32[]{:S(2)}) async-start(bf16[2,512,4,192]{1,0,3,2:T(2,128)(2,1)} %reshape.426), calls=%async_computation.2 | async-start | bytes 3145728 | tf_op jit(solution)/shard_map/all_to_all | solution.py:265
  404.4 530.8 %reduce-scatter.11.cloned.1.call-start = ((), (), s32[]{:S(2)}) async-start(), calls=%async_computation.15 | async-start | bytes 9732096 | tf_op jit(solution)/shard_map/reduce_scatter | solution.py:324
  417.8 542.7 %reduce-scatter.5.cloned.1.call-start = ((), (), s32[]{:S(2)}) async-start(), calls=%async_computation.12 | async-start | bytes 7299072 | tf_op jit(solution)/shard_map/reduce_scatter | solution.py:315
  428.2 134.0 %copy-start.5 = (bf16[2048,3,64]{0,2,1:T(8,128)(2,1)S(1)}, bf16[2048,3,64]{0,2,1:T(8,128)(2,1)}, u32[]{:S(2)}) copy-start(bf16[2048,3,64]{0,2,1:T(8,128)(2,1)} %copy-done.4) | copy-start | bytes 2359300
  428.2 134.0 %copy-start.8 = (f32[2048,3,64]{0,2,1:T(8,128)S(1)}, f32[2048,3,64]{0,2,1:T(8,128)}, u32[]{:S(2)}) copy-start(f32[2048,3,64]{0,2,1:T(8,128)} %custom-call.2) | copy-start | bytes 4718596
  431.1 7.3 copy-start
  443.3 11.7 %copy-start.1 = (f32[3,512,2048]{2,1,0:T(8,128)S(1)}, f32[3,512,2048]{2,1,0:T(8,128)}, u32[]{:S(2)}) copy-start(f32[3,512,2048]{2,1,0:T(8,128)} %copy-done) | copy-start | bytes 37748740 | tf_op jit(solution)/shard_map/while
  474.9 12.0 %copy-start.1 = (f32[3,512,2048]{2,1,0:T(8,128)S(1)}, f32[3,512,2048]{2,1,0:T(8,128)}, u32[]{:S(2)}) copy-start(f32[3,512,2048]{2,1,0:T(8,128)} %copy-done) | copy-start | bytes 37748740 | tf_op jit(solution)/shard_map/while
  495.2 7.3 copy-start
  507.5 12.8 %copy-start.1 = (f32[3,512,2048]{2,1,0:T(8,128)S(1)}, f32[3,512,2048]{2,1,0:T(8,128)}, u32[]{:S(2)}) copy-start(f32[3,512,2048]{2,1,0:T(8,128)} %copy-done) | copy-start | bytes 37748740 | tf_op jit(solution)/shard_map/while
  528.7 7.2 copy-start
  540.9 12.2 %copy-start.1 = (f32[3,512,2048]{2,1,0:T(8,128)S(1)}, f32[3,512,2048]{2,1,0:T(8,128)}, u32[]{:S(2)}) copy-start(f32[3,512,2048]{2,1,0:T(8,128)} %copy-done) | copy-start | bytes 37748740 | tf_op jit(solution)/shard_map/while
  571.8 9.9 %copy-start.23 = (bf16[4,512,3,64]{1,3,2,0:T(8,128)(2,1)S(1)}, bf16[4,512,3,64]{1,3,2,0:T(8,128)(2,1)}, u32[]{:S(2)}) copy-start(bf16[4,512,3,64]{1,3,2,0:T(8,128)(2,1)} %get-tuple-element.912) | copy-start | bytes 2359300 | tf_op jit(solution)/shard_map/while
  576.8 10.6 %copy-start.3 = (f32[3,512,2048]{2,1,0:T(8,128)S(1)}, f32[3,512,2048]{2,1,0:T(8,128)}, u32[]{:S(2)}) copy-start(f32[3,512,2048]{2,1,0:T(8,128)} %copy-done.2) | copy-start | bytes 37748740 | tf_op jit(solution)/shard_map/while
  601.8 9.4 copy-start.23
  606.8 10.1 %copy-start.3 = (f32[3,512,2048]{2,1,0:T(8,128)S(1)}, f32[3,512,2048]{2,1,0:T(8,128)}, u32[]{:S(2)}) copy-start(f32[3,512,2048]{2,1,0:T(8,128)} %copy-done.2) | copy-start | bytes 37748740 | tf_op jit(solution)/shard_map/while
  632.0 9.7 copy-start.23
  637.0 10.7 %copy-start.3 = (f32[3,512,2048]{2,1,0:T(8,128)S(1)}, f32[3,512,2048]{2,1,0:T(8,128)}, u32[]{:S(2)}) copy-start(f32[3,512,2048]{2,1,0:T(8,128)} %copy-done.2) | copy-start | bytes 37748740 | tf_op jit(solution)/shard_map/while
  662.9 9.4 copy-start.23
  667.8 10.8 %copy-start.3 = (f32[3,512,2048]{2,1,0:T(8,128)S(1)}, f32[3,512,2048]{2,1,0:T(8,128)}, u32[]{:S(2)}) copy-start(f32[3,512,2048]{2,1,0:T(8,128)} %copy-done.2) | copy-start | bytes 37748740 | tf_op jit(solution)/shard_map/while
  837.2 74.7 %copy-start.28 = (f32[1024,768]{1,0:T(8,128)S(1)}, f32[1024,768]{1,0:T(8,128)}, u32[]{:S(2)}) copy-start(f32[1024,768]{1,0:T(8,128)} %copy-done.26) | copy-start | bytes 9437188
  (36 other events, 145.9 us)
Sparse Core Ops, SparseCore 0:
  9.7 44.8 all-gather.5
  56.2 21.5 all-gather.7
  79.4 51.4 all-gather.9
  132.4 50.5 all-gather.11
  378.9 97.0 reduce-scatter.6
  482.8 134.5 reduce-scatter.8
  623.2 154.0 reduce-scatter.10
  837.4 123.1 reduce-scatter.4
where the time goes:
time: 990 us; the launch traced here: 980 us
  matrix products  337 us (34%)
  blocking collectives  218 us (22%)
  local copies, waits for them, and re-layouts  197 us (20%)
  other arithmetic  107 us (11%)
  waiting for transfers between devices  87.9 us (9%)
  between operations  17.3 us (2%)
  starting transfers between devices  13.8 us (1%)
    unnamed x3, blocking collectives  82.3 us
    all_to_all x1, blocking collectives, per_device(): lax.all_to_all(grad_qkv_heads, 'seq', split_axis=1, concat_axis=3, tiled=...  81.2 us
    all_to_all x1, waiting for transfers between devices, per_device(): lax.all_to_all(qkv_tok.reshape(seq_count, pos_count, 3, group_count, grou...  52.5 us
    dot_general x8, matrix products, one_block(): jnp.einsum('hbk,khd->bhd', grad_scores, keys_all, preferred_element_type=...  48.9 us
    dot_general x8, matrix products, one_block(): jnp.einsum('hbk,bhd->khd', attn_prob.astype(jnp.bfloat16), grad_blk, pref...  44.2 us
    dot_general x8, matrix products, one_block(): jnp.einsum('bhd,khd->hbk', grad_blk, values_all, preferred_element_type=j...  43 us
    dot_general x8, matrix products, one_block(): jnp.einsum('hbk,bhd->khd', grad_scores, query_blk, preferred_element_type...  41.9 us
    convert_element_type x8, other arithmetic, one_block(): grad_scores = (attn_prob * (grad_prob - row_dot)).astype(jnp.bfloat16)  39.8 us
  transfers between devices with their start and end apart: 11, of which 5 were waited for; matrix products, arithmetic and copies ran while one was open for 61% of the time, Pallas kernels for 0%

commit v1 on v0

v1 whole, which is shorter than its diff:
```python
import functools

import jax
import jax.numpy as jnp
from jax import lax
from jax.experimental import pallas as pl
from jax.experimental.pallas import tpu as pltpu
from jax.sharding import PartitionSpec as P

DH = 64
BLOCK_Q = 256
VMEM_LIMIT = 50 * 1024 * 1024
LOG2E = 1.4426950408889634
SCALE = DH ** (-0.5)


EPS = 1e-12
NEG_FILL = -1e30
HALF_ROOT = 0.7071067811865476
INV_ROOT_TAU = 0.3989422804014327


def dot_rows(left_op, right_op):
    return lax.dot_general(
        left_op, right_op, (((0,), (0,)), ((), ())), preferred_element_type=jnp.float32
    )


def dot_last(left_op, right_op):
    return lax.dot_general(
        left_op, right_op, (((1,), (1,)), ((), ())), preferred_element_type=jnp.float32
    )


def norm_forward(hidden, gain_vec, shift_vec):
    mean_val = jnp.mean(hidden, axis=-1, keepdims=True)
    centered = hidden - mean_val
    inv_std = lax.rsqrt(jnp.mean(centered * centered, axis=-1, keepdims=True) + EPS)
    normed = centered * inv_std
    return (normed * gain_vec + shift_vec, normed, inv_std)


def norm_backward(grad_out, normed, inv_std, gain_vec):
    grad_gain = jnp.sum(grad_out * normed, axis=0)
    grad_shift = jnp.sum(grad_out, axis=0)
    scaled = grad_out * gain_vec
    grad_in = inv_std * (
        scaled
        - jnp.mean(scaled, axis=-1, keepdims=True)
        - normed * jnp.mean(scaled * normed, axis=-1, keepdims=True)
    )
    return (grad_in, grad_gain, grad_shift)


def gelu_parts(pre_act):
    cdf_val = 0.5 * (1.0 + lax.erf(pre_act * HALF_ROOT))
    pdf_val = jnp.exp(-0.5 * pre_act * pre_act) * INV_ROOT_TAU
    return (pre_act * cdf_val, cdf_val + pre_act * pdf_val)


def split_three(val):
    hi = val.astype(jnp.bfloat16)
    rest = val - hi.astype(jnp.float32)
    mid = rest.astype(jnp.bfloat16)
    low = (rest - mid.astype(jnp.float32)).astype(jnp.bfloat16)
    return hi, mid, low


def lane_index(rows):
    return lax.broadcasted_iota(jnp.int32, (rows, DH), 1)


def pick_lanes(rows, columns):
    lanes = lane_index(rows)
    out = jnp.zeros((rows, DH), jnp.float32)
    for place, column in columns:
        out = jnp.where(lanes == place, column, out)
    return out.astype(jnp.bfloat16)


def build_keys(len_ref, qkv_ref, kx, vx, heads):
    width = heads * DH
    length = len_ref[0]
    groups, pos, _ = qkv_ref.shape
    for g in range(groups):
        rows = lax.broadcasted_iota(jnp.int32, (pos, DH), 0) + g * pos
        fill = jnp.where(rows < length, 0.0, NEG_FILL)
        lanes = lane_index(pos)
        extra = jnp.where(lanes == 0, fill, jnp.where(lanes < 4, 1.0, 0.0)).astype(jnp.bfloat16)
        ones = jnp.where(lanes < 3, 1.0, 0.0).astype(jnp.bfloat16)
        for h in range(heads):
            key = qkv_ref[g, :, width + h * DH : width + (h + 1) * DH]
            val = qkv_ref[g, :, 2 * width + h * DH : 2 * width + (h + 1) * DH]
            kx[h, g * pos : (g + 1) * pos, :] = jnp.concatenate([key, key, key, extra], axis=1)
            vx[h, g * pos : (g + 1) * pos, :] = jnp.concatenate([val, ones], axis=1)


def fwd_kernel(heads, len_ref, qkv_ref, out_ref, lse_ref, kx, vx):
    step = pl.program_id(0)
    pos = qkv_ref.shape[1]
    block = out_ref.shape[1]
    per = pos // block

    @pl.when(step == 0)
    def _():
        build_keys(len_ref, qkv_ref, kx, vx, heads)

    g = step // per
    start = pl.multiple_of((step % per) * block, block)
    query_all = qkv_ref[g, pl.ds(start, block), :]
    outs = []
    lses = []
    for h in range(heads):
        query = query_all[:, h * DH : (h + 1) * DH].astype(jnp.float32) * (SCALE * LOG2E)
        hi, mid, low = split_three(query)
        qx = jnp.concatenate([hi, mid, low, pick_lanes(block, [(0, 1.0)])], axis=1)
        scores = lax.dot_general(
            qx, kx[h], (((1,), (1,)), ((), ())), preferred_element_type=jnp.float32
        )
        row_max = jnp.max(scores, axis=1, keepdims=True)
        prob = jnp.exp2(scores - row_max).astype(jnp.bfloat16)
        both = jnp.dot(prob, vx[h], preferred_element_type=jnp.float32)
        row_sum = both[:, DH : DH + 1]
        outs.append((both[:, :DH] / row_sum).astype(jnp.bfloat16))
        lses.append(row_max + jnp.log2(row_sum))
    out_ref[0] = jnp.concatenate(outs, axis=1)
    lanes = lax.broadcasted_iota(jnp.int32, (block, 128), 1)
    keep = jnp.zeros((block, 128), jnp.float32)
    for h in range(heads):
        keep = jnp.where(lanes == h, lses[h], keep)
    lse_ref[...] = keep


def attend_forward(qkv, length):
    groups, pos, cols = qkv.shape
    heads = (cols // 3) // DH
    full = groups * pos
    block = min(BLOCK_Q, pos)
    per = pos // block
    return pl.pallas_call(
        functools.partial(fwd_kernel, heads),
        grid=(full // block,),
        in_specs=[
            pl.BlockSpec(memory_space=pltpu.SMEM),
            pl.BlockSpec((groups, pos, cols), lambda i: (0, 0, 0)),
        ],
        out_specs=[
            pl.BlockSpec((1, block, heads * DH), lambda i: (i // per, i % per, 0)),
            pl.BlockSpec((block, 128), lambda i: (i, 0)),
        ],
        out_shape=[
            jax.ShapeDtypeStruct((groups, pos, heads * DH), jnp.bfloat16),
            jax.ShapeDtypeStruct((full, 128), jnp.float32),
        ],
        scratch_shapes=[
            pltpu.VMEM((heads, full, 4 * DH), jnp.bfloat16),
            pltpu.VMEM((heads, full, 2 * DH), jnp.bfloat16),
        ],
        compiler_params=pltpu.CompilerParams(vmem_limit_bytes=VMEM_LIMIT),
        cost_estimate=pl.CostEstimate(
            flops=heads * full * full * 4 * DH * 4,
            bytes_accessed=groups * pos * cols * 2,
            transcendentals=heads * full * full,
        ),
    )(length, qkv)


def bwd_kernel(heads, len_ref, qkv_ref, grad_ref, att_ref, lse_ref, out_ref, kx, vx, dk, dv):
    step = pl.program_id(0)
    steps = pl.num_programs(0)
    groups, pos, cols = qkv_ref.shape
    block = lse_ref.shape[0]
    per = pos // block
    width = heads * DH

    @pl.when(step == 0)
    def _():
        build_keys(len_ref, qkv_ref, kx, vx, heads)
        dk[...] = jnp.zeros_like(dk)
        dv[...] = jnp.zeros_like(dv)

    g = step // per
    start = pl.multiple_of((step % per) * block, block)
    query_all = qkv_ref[g, pl.ds(start, block), :]
    grad_all = grad_ref[g, pl.ds(start, block), :]
    att_all = att_ref[g, pl.ds(start, block), :]
    outs = []
    for h in range(heads):
        raw = query_all[:, h * DH : (h + 1) * DH]
        hi, mid, low = split_three(raw.astype(jnp.float32) * (SCALE * LOG2E))
        a, b, c = split_three(-lse_ref[:, h : h + 1])
        f32 = jnp.float32
        extra = pick_lanes(
            block, [(0, 1.0), (1, a.astype(f32)), (2, b.astype(f32)), (3, c.astype(f32))]
        )
        qx = jnp.concatenate([hi, mid, low, extra], axis=1)
        grad = grad_all[:, h * DH : (h + 1) * DH]
        att = att_all[:, h * DH : (h + 1) * DH]
        row_dot = jnp.sum(grad.astype(f32) * att.astype(f32), axis=1, keepdims=True)
        a, b, c = split_three(-row_dot)
        extra = pick_lanes(block, [(0, a.astype(f32)), (1, b.astype(f32)), (2, c.astype(f32))])
        gx = jnp.concatenate([grad, extra], axis=1)
        prob = jnp.exp2(
            lax.dot_general(kx[h], qx, (((1,), (1,)), ((), ())), preferred_element_type=f32)
        )
        diff = lax.dot_general(vx[h], gx, (((1,), (1,)), ((), ())), preferred_element_type=f32)
        grad_scores = (prob * diff).astype(jnp.bfloat16)
        dv[h] += jnp.dot(prob.astype(jnp.bfloat16), grad, preferred_element_type=f32)
        dk[h] += jnp.dot(grad_scores, raw, preferred_element_type=f32)
        grad_query = lax.dot_general(
            grad_scores, kx[h, :, :DH], (((0,), (0,)), ((), ())), preferred_element_type=f32
        )
        outs.append((grad_query * SCALE).astype(jnp.bfloat16))
    out_ref[g, pl.ds(start, block), 0:width] = jnp.concatenate(outs, axis=1)

    @pl.when(step == steps - 1)
    def _():
        for p in range(groups):
            rows = slice(p * pos, (p + 1) * pos)
            parts = [(dk[h, rows, :] * SCALE).astype(jnp.bfloat16) for h in range(heads)]
            parts += [dv[h, rows, :].astype(jnp.bfloat16) for h in range(heads)]
            if cols > 3 * width:
                parts.append(jnp.zeros((pos, cols - 3 * width), jnp.bfloat16))
            out_ref[p, :, width:] = jnp.concatenate(parts, axis=1)


def attend_backward(qkv, grad, att, lse, length):
    groups, pos, cols = qkv.shape
    heads = (cols // 3) // DH
    full = groups * pos
    block = min(BLOCK_Q, pos)
    whole = lambda last: pl.BlockSpec((groups, pos, last), lambda i: (0, 0, 0))
    return pl.pallas_call(
        functools.partial(bwd_kernel, heads),
        grid=(full // block,),
        in_specs=[
            pl.BlockSpec(memory_space=pltpu.SMEM),
            whole(cols),
            whole(heads * DH),
            whole(heads * DH),
            pl.BlockSpec((block, 128), lambda i: (i, 0)),
        ],
        out_specs=whole(cols),
        out_shape=jax.ShapeDtypeStruct((groups, pos, cols), jnp.bfloat16),
        scratch_shapes=[
            pltpu.VMEM((heads, full, 4 * DH), jnp.bfloat16),
            pltpu.VMEM((heads, full, 2 * DH), jnp.bfloat16),
            pltpu.VMEM((heads, full, DH), jnp.float32),
            pltpu.VMEM((heads, full, DH), jnp.float32),
        ],
        compiler_params=pltpu.CompilerParams(vmem_limit_bytes=VMEM_LIMIT),
        cost_estimate=pl.CostEstimate(
            flops=heads * full * full * 4 * DH * 10,
            bytes_accessed=groups * pos * cols * 4,
            transcendentals=heads * full * full,
        ),
    )(length, qkv, grad, att, lse)


def project_kernel(tok_ref, weight_ref, bias_ref, out_ref):
    out_ref[0] = (
        jnp.dot(tok_ref[...], weight_ref[...], preferred_element_type=jnp.float32) + bias_ref[...]
    ).astype(jnp.bfloat16)


def project_groups(tokens, weight, bias, groups):
    rows, depth = tokens.shape
    cols = weight.shape[1] // groups
    return pl.pallas_call(
        project_kernel,
        grid=(groups,),
        in_specs=[
            pl.BlockSpec((rows, depth), lambda g: (0, 0)),
            pl.BlockSpec((depth, cols), lambda g: (0, g)),
            pl.BlockSpec((1, cols), lambda g: (0, g)),
        ],
        out_specs=pl.BlockSpec((1, rows, cols), lambda g: (g, 0, 0)),
        out_shape=jax.ShapeDtypeStruct((groups, rows, cols), jnp.bfloat16),
        compiler_params=pltpu.CompilerParams(vmem_limit_bytes=VMEM_LIMIT),
        cost_estimate=pl.CostEstimate(
            flops=2 * rows * depth * cols * groups,
            bytes_accessed=2 * (rows * depth + depth * cols * groups + rows * cols * groups),
            transcendentals=0,
        ),
    )(tokens, weight, bias)


def input_grad_kernel(gq_ref, weight_ref, base_ref, out_ref):
    groups, _, cols = gq_ref.shape
    total = base_ref[...]
    for g in range(groups):
        total += lax.dot_general(
            gq_ref[g],
            weight_ref[:, g * cols : (g + 1) * cols],
            (((1,), (1,)), ((), ())),
            preferred_element_type=jnp.float32,
        )
    out_ref[...] = total.astype(jnp.bfloat16)


def input_grad(grad_qkv, weight, base):
    groups, rows, cols = grad_qkv.shape
    depth = weight.shape[0]
    block = min(256, rows)
    return pl.pallas_call(
        input_grad_kernel,
        grid=(rows // block,),
        in_specs=[
            pl.BlockSpec((groups, block, cols), lambda i: (0, i, 0)),
            pl.BlockSpec(weight.shape, lambda i: (0, 0)),
            pl.BlockSpec((block, depth), lambda i: (i, 0)),
        ],
        out_specs=pl.BlockSpec((block, depth), lambda i: (i, 0)),
        out_shape=jax.ShapeDtypeStruct((rows, depth), jnp.bfloat16),
        compiler_params=pltpu.CompilerParams(vmem_limit_bytes=VMEM_LIMIT),
        cost_estimate=pl.CostEstimate(
            flops=2 * rows * depth * cols * groups,
            bytes_accessed=2 * (3 * rows * depth + depth * cols * groups + rows * cols * groups),
            transcendentals=0,
        ),
    )(grad_qkv, weight, base)


def swap_groups(arr):
    return lax.all_to_all(arr, "seq", split_axis=0, concat_axis=0, tiled=True)


def sum_groups(share):
    groups = lax.axis_size("seq")
    if groups != 4:
        return jnp.sum(lax.all_gather(share, "seq", axis=0).astype(jnp.float32), axis=0)
    others = [
        lax.ppermute(share, "seq", [(i, i ^ k) for i in range(groups)]).astype(jnp.float32)
        for k in (1, 2, 3)
    ]
    return (share.astype(jnp.float32) + others[0]) + (others[1] + others[2])


def reduce_rows(grad):
    share = lax.psum_scatter(grad.astype(jnp.bfloat16), "shard", scatter_dimension=0, tiled=True)
    return sum_groups(share)


def reduce_with(grad, vectors):
    rows = grad.shape[0]
    columns = jnp.concatenate([vec.reshape(rows, -1) for vec in vectors], axis=1)
    columns = jnp.pad(columns, ((0, 0), (0, -columns.shape[1] % 128)))
    total = reduce_rows(jnp.concatenate([grad, columns], axis=1))
    outs = [total[:, : grad.shape[1]]]
    start = grad.shape[1]
    for vec in vectors:
        count = vec.shape[0] // rows
        outs.append(total[:, start : start + count].reshape(-1))
        start += count
    return outs


def per_device(
    hidden_in,
    seq_lengths,
    w_qkv,
    b_query,
    b_value,
    w_out,
    b_out,
    ln1_gain,
    ln1_bias,
    w_up,
    b_up,
    w_down,
    b_down,
    ln2_gain,
    ln2_bias,
    cotangent,
):
    groups = lax.axis_size("seq")
    shard_count = lax.axis_size("shard")
    seq_count, pos, model_width = hidden_in.shape
    tok_count = seq_count * pos
    width = model_width // groups
    cols = -(-3 * width // 128) * 128
    f32 = jnp.float32
    small = (b_query, b_value, b_out, ln1_gain, ln1_bias, b_down, ln2_gain, ln2_bias, b_up)
    packed = lax.all_gather(jnp.concatenate(small), "shard", axis=0)
    full_small = []
    start = 0
    for vec in small:
        full_small.append(packed[:, start : start + vec.shape[0]].reshape(-1).astype(f32))
        start += vec.shape[0]
    (
        query_bias,
        value_bias,
        out_bias,
        gain_one,
        shift_one,
        down_bias,
        gain_two,
        shift_two,
        up_bias,
    ) = full_small
    by_group = jnp.swapaxes(w_qkv.reshape(w_qkv.shape[0], 3, groups, width), 1, 2).reshape(
        w_qkv.shape[0], groups, 3 * width
    )
    by_group = jnp.pad(by_group, ((0, 0), (0, 0), (0, cols - 3 * width)))
    qkv_weight = lax.all_gather(
        by_group.reshape(w_qkv.shape[0], groups * cols), "shard", axis=0, tiled=True
    )
    out_weight = lax.all_gather(w_out, "shard", axis=0, tiled=True)
    up_weight = lax.all_gather(w_up, "shard", axis=0, tiled=True)
    down_weight = lax.all_gather(w_down, "shard", axis=0, tiled=True)
    bias = jnp.stack([query_bias, jnp.zeros_like(query_bias), value_bias])
    bias = jnp.swapaxes(bias.reshape(3, groups, width), 0, 1).reshape(groups, 3 * width)
    bias = jnp.pad(bias, ((0, 0), (0, cols - 3 * width))).reshape(1, groups * cols)
    tokens = hidden_in.reshape(tok_count, model_width)
    lengths = [seq_lengths[n : n + 1] for n in range(seq_count)]
    qkv = [
        swap_groups(project_groups(hidden_in[n], qkv_weight, bias, groups))
        for n in range(seq_count)
    ]
    att = []
    lse = []
    arrived = []
    for n in range(seq_count):
        att_n, lse_n = attend_forward(qkv[n], lengths[n])
        att.append(att_n)
        lse.append(lse_n)
        arrived.append(swap_groups(att_n))
    attended = jnp.concatenate(
        [jnp.swapaxes(arr, 0, 1).reshape(pos, model_width) for arr in arrived]
    )
    projected = jnp.dot(attended, out_weight, preferred_element_type=f32) + out_bias
    ln_one, normed_one, inv_one = norm_forward(
        tokens.astype(f32) + projected, gain_one, shift_one
    )
    ln_low = ln_one.astype(jnp.bfloat16)
    pre_act = jnp.dot(ln_low, up_weight, preferred_element_type=f32) + up_bias
    act_val, act_slope = gelu_parts(pre_act)
    act_low = act_val.astype(jnp.bfloat16)
    ffn_out = jnp.dot(act_low, down_weight, preferred_element_type=f32) + down_bias
    result, normed_two, inv_two = norm_forward(ln_one + ffn_out, gain_two, shift_two)
    output = result.astype(jnp.bfloat16).reshape(seq_count, pos, model_width)
    grad_y = cotangent.reshape(tok_count, model_width).astype(f32)
    grad_two, grad_gain_two, grad_shift_two = norm_backward(grad_y, normed_two, inv_two, gain_two)
    grad_ffn = grad_two.astype(jnp.bfloat16)
    grad_down_bias = jnp.sum(grad_ffn, axis=0, dtype=f32)
    grad_down = reduce_rows(dot_rows(act_low, grad_ffn))
    grad_pre = (dot_last(grad_ffn, down_weight) * act_slope).astype(jnp.bfloat16)
    grad_up_bias = jnp.sum(grad_pre, axis=0, dtype=f32)
    grad_up = reduce_rows(dot_rows(ln_low, grad_pre))
    grad_ln = dot_last(grad_pre, up_weight) + grad_two
    grad_one, grad_gain_one, grad_shift_one = norm_backward(grad_ln, normed_one, inv_one, gain_one)
    grad_proj = grad_one.astype(jnp.bfloat16)
    grad_out_bias = jnp.sum(grad_proj, axis=0, dtype=f32)
    (
        grad_out,
        sum_out_bias,
        sum_gain_one,
        sum_shift_one,
        sum_down_bias,
        sum_gain_two,
        sum_shift_two,
        sum_up_bias,
    ) = reduce_with(
        dot_rows(attended, grad_proj),
        (
            grad_out_bias,
            grad_gain_one,
            grad_shift_one,
            grad_down_bias,
            grad_gain_two,
            grad_shift_two,
            grad_up_bias,
        ),
    )
    grad_att = dot_last(grad_proj, out_weight).astype(jnp.bfloat16)
    grad_att = grad_att.reshape(seq_count, pos, groups, width)
    grad_heads = [swap_groups(jnp.swapaxes(grad_att[n], 0, 1)) for n in range(seq_count)]
    back = [
        swap_groups(attend_backward(qkv[n], grad_heads[n], att[n], lse[n], lengths[n]))
        for n in range(seq_count)
    ]
    grad_base = grad_one.reshape(seq_count, pos, model_width)
    grad_input = jnp.stack(
        [input_grad(back[n], qkv_weight, grad_base[n]) for n in range(seq_count)]
    )
    grad_qkv = jnp.concatenate(back, axis=1)[:, :, : 3 * width]
    by_part = [dot_rows(tokens, grad_qkv[g]) for g in range(groups)]
    grad_w = jnp.stack(by_part, axis=1).reshape(model_width, groups, 3, width)
    grad_w = jnp.swapaxes(grad_w, 1, 2).reshape(model_width, 3 * model_width)
    col_sum = jnp.sum(grad_qkv, axis=1, dtype=f32).reshape(groups, 3, width)
    grad_w, sum_query_bias, sum_value_bias = reduce_with(
        grad_w, (col_sum[:, 0].reshape(-1), col_sum[:, 2].reshape(-1))
    )
    return (
        output,
        grad_input,
        grad_w,
        sum_query_bias,
        sum_value_bias,
        grad_out,
        sum_out_bias,
        sum_gain_one,
        sum_shift_one,
        grad_up,
        sum_up_bias,
        grad_down,
        sum_down_bias,
        sum_gain_two,
        sum_shift_two,
    )


def solution(mesh):
    in_specs = (
        P("shard", "seq", None),
        P("shard"),
        P("shard", None),
        P("shard"),
        P("shard"),
        P("shard", None),
        P("shard"),
        P("shard"),
        P("shard"),
        P("shard", None),
        P("shard"),
        P("shard", None),
        P("shard"),
        P("shard"),
        P("shard"),
        P("shard", "seq", None),
    )
    out_specs = (
        P("shard", "seq", None),
        P("shard", "seq", None),
        P("shard", None),
        P("shard"),
        P("shard"),
        P("shard", None),
        P("shard"),
        P("shard"),
        P("shard"),
        P("shard", None),
        P("shard"),
        P("shard", None),
        P("shard"),
        P("shard"),
        P("shard"),
    )
    return jax.shard_map(
        per_device, mesh=mesh, in_specs=in_specs, out_specs=out_specs, check_vma=False
    )
```

time: 990 us -> 553 us (0.56)
  matrix products: 337 us -> 78.8 us
  blocking collectives: 218 us -> 15.7 us
  Pallas kernels: 0 us -> 155 us
  local copies, waits for them, and re-layouts: 197 us -> 46.4 us
  other arithmetic: 107 us -> 26.7 us
  waiting for transfers between devices: 87.9 us -> 156 us
  starting transfers between devices: 13.8 us -> 48.9 us
    dot_general x60 -> x3, matrix products: 282 us -> 25.4 us  [the longest x1 12.4 us: per_device(): pre_act = jnp.dot(ln_low, up_weight, preferred_element_type=f32) + up_bias]
    pallas_call x0 -> x8, Pallas kernels: none -> 155 us  [the longest x2 85.7 us: attend_backward(): pl.pallas_call(functools.partial(bwd_kernel, heads), grid=(full // block,...]
    unnamed x3 -> x0, blocking collectives: 82.3 us -> none
    all_to_all x1 -> x0, blocking collectives: 81.2 us -> none  [per_device(): lax.all_to_all(grad_qkv_heads, 'seq', split_axis=1, concat_axis=3, tiled=...]
    ppermute x0 -> x12, waiting for transfers between devices: none -> 62.8 us  [sum_groups(): lax.ppermute(share, 'seq', [(i, i ^ k) for i in range(groups)])]
    convert_element_type x33 -> x2, other arithmetic: 52.2 us -> 0.08 us  [per_device(): packed[:, start:start + vec.shape[0]].reshape(-1).astype(f32)]
    another operation x18 -> x4, local copies, waits for them, and re-layouts: 44 us -> 0.33 us  [the longest x2 0.17 us: reduce_with(): vec.reshape(rows, -1)]
    all_gather x5 -> x1, blocking collectives: 55 us -> 15.7 us  [per_device(): packed = lax.all_gather(jnp.concatenate(small), 'shard', axis=0)]
  transfers between devices with their start and end apart: 11 -> 28, of which waited for: 5 -> 10; matrix products, arithmetic and copies ran while one was open for 61% -> 17% of each run, Pallas kernels for 0% -> 29%
where the time goes in v1:
time: 553 us; the launch traced here: 543 us
  waiting for transfers between devices  156 us (28%)
  Pallas kernels  155 us (28%)
  matrix products  78.8 us (14%)
  starting transfers between devices  48.9 us (9%)
  local copies, waits for them, and re-layouts  46.4 us (8%)
  other arithmetic  26.7 us (5%)
  blocking collectives  15.7 us (3%)
  between operations  15.5 us (3%)
    pallas_call x2, Pallas kernels, attend_backward(): pl.pallas_call(functools.partial(bwd_kernel, heads), grid=(full // block,...  85.7 us
    ppermute x12, waiting for transfers between devices, sum_groups(): lax.ppermute(share, 'seq', [(i, i ^ k) for i in range(groups)])  62.8 us
    all_to_all x8, waiting for transfers between devices, swap_groups(): return lax.all_to_all(arr, 'seq', split_axis=0, concat_axis=0, tiled=True)  61.5 us
    pallas_call x2, Pallas kernels, attend_forward(): pl.pallas_call(functools.partial(fwd_kernel, heads), grid=(full // block,...  46.5 us
    all_to_all x8, starting transfers between devices, swap_groups(): return lax.all_to_all(arr, 'seq', split_axis=0, concat_axis=0, tiled=True)  33 us
    dot_general x7, matrix products, dot_rows(): lax.dot_general(left_op, right_op, (((0,), (0,)), ((), ())), preferred_el...  31.2 us
    all_gather x1, waiting for transfers between devices, per_device(): lax.all_gather(by_group.reshape(w_qkv.shape[0], groups * cols), 'shard',...  29.7 us
    unnamed x78, local copies, waits for them, and re-layouts  23.5 us
  transfers between devices with their start and end apart: 28, of which 10 were waited for; matrix products, arithmetic and copies ran while one was open for 17% of the time, Pallas kernels for 29%

profile of v1, /device:TPU:0, one launch (start us, length us, event | category | flops | bytes accessed | tf_op | source)
XLA Modules:
  0.0 543.3 jit_solution(12564729867065315320)
XLA Ops:
  12.7 15.7 %all-gather.1 = bf16[8,1,1152]{2,1,0:T(2,128)(2,1)S(1)} all-gather(bf16[1,1,1152]{2,1,0:T(2,128)(2,1)S(1)} %reshape.323), channel_id=2, replica_groups=mesh['seq'=4,'shard'=8] {'shard'}, dimensions={0}, use_global_device_ids=true | all-gather | bytes 20736 | tf_op jit(solution)/shard_map/all_gather | solution.py:384
  29.1 29.7 %all-gather.7.cloned.1.call-done.weight_ref = bf16[768,2560]{1,0:T(8,128)(2,1)} async-done(((bf16[96,2560]{1,0:T(8,128)(2,1)}), bf16[768,2560]{1,0:T(8,128)(2,1)}) %all-gather.7.cloned.1.call-update) | async-done | bytes 3932176 | tf_op jit(solution)/shard_map/all_gather | solution.py:405
  58.8 5.9 %shard_map.271 = bf16[4,512,640]{2,1,0:T(8,128)(2,1)} custom-call(bf16[512,768]{1,0:T(8,128)(2,1)S(1)} %get-tuple-element.100.tok_ref, bf16[768,2560]{1,0:T(8,128)(2,1)} %all-gather.7.cloned.1.call-done.weight_ref, f32[1,2560]{1,0:T(1,128)S(1)} %bitcast.122), custom_call_target="tpu_custom_call" | custom-call | flops 2013265920 | bytes 7340032 | tf_op jit(solution)/shard_map/pallas_call | solution.py:269
  64.7 3.7 all-to-all-start
  69.0 6.0 %shard_map.273 = bf16[4,512,640]{2,1,0:T(8,128)(2,1)} custom-call(bf16[512,768]{1,0:T(8,128)(2,1)S(1)} %get-tuple-element.101.tok_ref, bf16[768,2560]{1,0:T(8,128)(2,1)} %all-gather.7.cloned.1.call-done.weight_ref, f32[1,2560]{1,0:T(1,128)S(1)} %bitcast.123), custom_call_target="tpu_custom_call" | custom-call | flops 2013265920 | bytes 7340032 | tf_op jit(solution)/shard_map/pallas_call | solution.py:269
  74.9 24.6 %all-to-all-done.qkv_ref = bf16[4,512,640]{2,1,0:T(8,128)(2,1)S(1)} async-done(((bf16[4,512,640]{2,1,0:T(8,128)(2,1)}), bf16[4,512,640]{2,1,0:T(8,128)(2,1)S(1)}, u32[]{:S(2)}, u32[]{:S(2)}) %all-to-all-start) | async-done | bytes 2621472 | tf_op jit(solution)/shard_map/all_to_all | solution.py:325
  99.6 4.6 all-to-all-start.2
  105.0 23.3 %shard_map.272 = (bf16[4,512,192]{2,1,0:T(8,128)(2,1)S(1)}, f32[2048,128]{1,0:T(8,128)S(1)}) custom-call(s32[1]{0:T(128)} %get-tuple-element.118.len_ref, bf16[4,512,640]{2,1,0:T(8,128)(2,1)} %copy-done.11), custom_call_target="tpu_custom_call" | custom-call | flops 12884901888 | bytes 2621440 | tf_op jit(solution)/shard_map/pallas_call | solution.py:140
  130.4 4.3 all-to-all-done.2.qkv_ref
  134.7 3.5 all-to-all-start.1
  138.2 23.2 %shard_map.274 = (bf16[4,512,192]{2,1,0:T(8,128)(2,1)S(1)}, f32[2048,128]{1,0:T(8,128)S(1)}) custom-call(s32[1]{0:T(128)} %get-tuple-element.119.len_ref, bf16[4,512,640]{2,1,0:T(8,128)(2,1)} %all-to-all-done.2.qkv_ref), custom_call_target="tpu_custom_call" | custom-call | flops 12884901888 | bytes 2621440 | tf_op jit(solution)/shard_map/pallas_call | solution.py:140
  163.6 4.2 all-to-all-start.3
  172.0 6.2 %all-to-all-done.3 = bf16[4,512,192]{1,2,0:T(8,128)(2,1)} async-done(((bf16[4,512,192]{1,2,0:T(8,128)(2,1)}), bf16[4,512,192]{1,2,0:T(8,128)(2,1)}, u32[]{:S(2)}, u32[]{:S(2)}) %all-to-all-start.3) | async-done | bytes 786464 | tf_op jit(solution)/shard_map/all_to_all | solution.py:325
  178.2 3.7 fusion.32
  184.2 12.4 %multiply_convert_fusion = (bf16[1024,3072]{1,0:T(8,128)(2,1)}, f32[1024,3072]{1,0:T(8,128)}) fusion(f32[3072]{0:T(1024)S(1)} %reshape.316, bf16[768,3072]{1,0:T(8,128)(2,1)} %all-gather.11.cloned.1.call-done, f32[1024,768]{1,0:T(8,128)} %copy-done.6, f32[768]{0:T(1024)S(1)} %reshape.315, f32[768]{0:T(1024)S(1)} %reshape.314, f32[1024]{0:T(1024)S(1)} %add_rsqrt_fusion.1, ...), kind=kOutput, calls=%fused_computation.7 | convolution fusion | flops 4854644736 | bytes 26765312 | tf_op jit(solution)/shard_map/dot_general | solution.py:436
  196.6 9.3 %fusion.33 = (f32[1024]{0:T(1024)S(1)}, f32[1024,768]{1,0:T(8,128)S(1)}) fusion(f32[768]{0:T(1024)S(1)} %reshape.317, bf16[1024,3072]{1,0:T(8,128)(2,1)} %get-tuple-element.122, bf16[3072,768]{1,0:T(8,128)(2,1)} %all-gather.13.cloned.1.call-done, f32[768]{0:T(1024)S(1)} %reshape.315, f32[768]{0:T(1024)S(1)} %reshape.314, f32[1024]{0:T(1024)S(1)} %add_rsqrt_fusion.1, ...), kind=kOutput, calls=%fused_computation.108 | convolution fusion | flops 4837342208 | bytes 17323008 | tf_op jit(solution)/shard_map/dot_general | solution.py:439
  207.3 2.7 fusion.12
  211.3 12.9 %fusion.34 = (bf16[3072]{0:T(1024)(128)(2,1)S(1)}, bf16[1024,3072]{1,0:T(8,128)(2,1)S(1)}) fusion(f32[1024,3072]{1,0:T(8,128)} %get-tuple-element.123, f32[3072]{0:T(1024)S(1)} %reshape.316, bf16[3072,768]{1,0:T(8,128)(2,1)S(1)} %bitcast.147, f32[1024,768]{1,0:T(8,128)S(1)} %get-tuple-element.92), kind=kOutput, calls=%fused_computation.109 | convolution fusion | flops 4870370304 | bytes 26757120 | tf_op jit(solution)/shard_map/dot_general | solution.py:30
  224.2 6.1 %multiply_reduce_fusion = (bf16[768]{0:T(1024)(128)(2,1)S(1)}, f32[1024]{0:T(1024)S(1)}, f32[1024]{0:T(1024)S(1)}, bf16[768]{0:T(1024)(128)(2,1)S(1)}, f32[1024,768]{1,0:T(8,128)S(1)}) fusion(f32[1024,768]{1,0:T(8,128)S(1)} %copy-done.7, f32[1024]{0:T(1024)S(1)} %add_rsqrt_fusion.1, f32[1024]{0:T(1024)S(1)} %broadcast_multiply_fusion.4, ...), kind=kOutput, calls=%fused_computation.24 | convolution fusion | flops 4839698432 | bytes 20469760 | tf_op jit(solution)/shard_map/dot_general | solution.py:30
  230.3 2.7 convert_reduce_fusion
  233.6 4.6 convolution_convert_fusion.3
  241.4 10.4 %convolution_convert_fusion.1 = bf16[768,3072]{1,0:T(8,128)(2,1)} fusion(bf16[1024,3072]{1,0:T(8,128)(2,1)} %copy-done.28, f32[1024,768]{1,0:T(8,128)} %copy-done.6, f32[768]{0:T(1024)S(1)} %reshape.315, f32[768]{0:T(1024)S(1)} %reshape.314, f32[1024]{0:T(1024)S(1)} %add_rsqrt_fusion.1, f32[1024]{0:T(1024)S(1)} %broadcast_multiply_fusion.4), kind=kOutput, calls=%fused_computation.11 | convolution fusion | flops 4838129664 | bytes 14170112 | tf_op jit(solution)/shard_map/dot_general | solution.py:24
  253.1 3.3 convolution_convert_fusion.2
  257.7 3.5 all-to-all-start.4
  261.3 9.6 %convolution_convert_fusion = bf16[3072,768]{1,0:T(8,128)(2,1)} fusion(bf16[1024,3072]{1,0:T(8,128)(2,1)} %get-tuple-element.122, f32[1024,768]{1,0:T(8,128)} %copy-done.10), kind=kOutput, calls=%fused_computation.10 | convolution fusion | flops 4834983936 | bytes 14155776 | tf_op jit(solution)/shard_map/dot_general | solution.py:24
  272.3 4.4 all-to-all-start.6
  279.5 42.9 %shard_map.275 = bf16[4,512,640]{2,1,0:T(8,128)(2,1)} custom-call(s32[1]{0:T(128)} %get-tuple-element.118.len_ref, bf16[4,512,640]{2,1,0:T(8,128)(2,1)} %copy-done.11, bf16[4,512,192]{2,1,0:T(8,128)(2,1)S(1)} %copy.76.grad_ref, bf16[4,512,192]{2,1,0:T(8,128)(2,1)S(1)} %get-tuple-element.19.att_ref, f32[2048,128]{1,0:T(8,128)S(1)} %copy-done.3), custom_call_target="tpu_custom_call" | custom-call | flops 32212254720 | bytes 5242880 | tf_op jit(solution)/shard_map/pallas_call | solution.py:233
  322.3 5.0 all-to-all-start.5
  328.8 42.9 %shard_map.277 = bf16[4,512,640]{2,1,0:T(8,128)(2,1)} custom-call(s32[1]{0:T(128)} %get-tuple-element.119.len_ref, bf16[4,512,640]{2,1,0:T(8,128)(2,1)} %all-to-all-done.2.qkv_ref, bf16[4,512,192]{2,1,0:T(8,128)(2,1)S(1)} %copy.77.grad_ref, bf16[4,512,192]{2,1,0:T(8,128)(2,1)S(1)} %get-tuple-element.20.att_ref, f32[2048,128]{1,0:T(8,128)S(1)} %copy-done.1), custom_call_target="tpu_custom_call" | custom-call | flops 32212254720 | bytes 5242880 | tf_op jit(solution)/shard_map/pallas_call | solution.py:233
  371.6 4.2 all-to-all-start.7
  376.1 3.5 constant_dynamic-update-slice_fusion.1
  379.6 25.8 %all-to-all-done.7.gq_ref = bf16[4,512,640]{2,1,0:T(8,128)(2,1)S(1)} async-done(((bf16[4,512,640]{2,1,0:T(8,128)(2,1)}), bf16[4,512,640]{2,1,0:T(8,128)(2,1)S(1)}, u32[]{:S(2)}, u32[]{:S(2)}) %all-to-all-start.7) | async-done | bytes 2621472 | tf_op jit(solution)/shard_map/all_to_all | solution.py:325
  405.4 1.9 constant_dynamic-update-slice_fusion
  407.3 3.3 slice_reduce_fusion
  410.9 3.1 convolution_convert_fusion.7
  419.0 2.0 pad_maximum_fusion
  421.0 6.1 %copy.93 = bf16[768,2432]{1,0:T(8,128)(2,1)} copy(bf16[768,2432]{0,1:T(8,128)(2,1)} %pad_maximum_fusion) | data formatting | bytes 7471104
  427.2 2.1 fusion.29
  429.3 5.7 %shard_map.276 = bf16[512,768]{1,0:T(8,128)(2,1)S(1)} custom-call(bf16[4,512,640]{2,1,0:T(8,128)(2,1)} %all-to-all-done.5.gq_ref, bf16[768,2560]{1,0:T(8,128)(2,1)} %all-gather.7.cloned.1.call-done.weight_ref, f32[512,768]{1,0:T(8,128)S(1)} %get-tuple-element.96.base_ref), custom_call_target="tpu_custom_call" | custom-call | flops 2013265920 | bytes 8912896 | tf_op jit(solution)/shard_map/pallas_call | solution.py:305
  437.8 1.8 collective-permute-start.5
  439.6 5.4 shard_map.278
  446.8 1.8 collective-permute-start.8
  456.3 41.7 %collective-permute-done.10 = bf16[384,768]{1,0:T(8,128)(2,1)} collective-permute-done((bf16[384,768]{1,0:T(8,128)(2,1)}, bf16[384,768]{1,0:T(8,128)(2,1)}, u32[]{:S(2)}, u32[]{:S(2)}) %collective-permute-start.10) | collective-permute-done | bytes 589856 | tf_op jit(solution)/shard_map/ppermute | solution.py:333
  503.1 2.7 add_add_fusion.4
  505.9 8.3 %collective-permute-done.9 = bf16[384,768]{1,0:T(8,128)(2,1)S(1)} collective-permute-done((bf16[384,768]{1,0:T(8,128)(2,1)S(1)}, bf16[384,768]{1,0:T(8,128)(2,1)S(1)}, u32[]{:S(2)}, u32[]{:S(2)}) %collective-permute-start.9) | collective-permute-done | bytes 589856 | tf_op jit(solution)/shard_map/ppermute | solution.py:333
  514.2 2.3 add_add_fusion.3
  516.9 7.4 %collective-permute-done = bf16[96,2432]{1,0:T(8,128)(2,1)} collective-permute-done((bf16[96,2432]{1,0:T(8,128)(2,1)}, bf16[96,2432]{1,0:T(8,128)(2,1)}, u32[]{:S(2)}, u32[]{:S(2)}) %collective-permute-start) | collective-permute-done | bytes 466976 | tf_op jit(solution)/shard_map/ppermute | solution.py:333
  527.1 5.3 collective-permute-done.2
  (193 shorter events, 61.9 us)
Async XLA Ops:
  7.2 5.4 copy-start.19
  7.2 5.4 copy-start.20
  7.2 5.4 copy-start.21
  7.2 5.4 copy-start.22
  7.2 5.4 copy-start.23
  7.2 5.4 copy-start.18
  7.2 5.4 copy-start.24
  7.3 5.4 copy-start.25
  7.3 5.4 copy-start.26
  7.3 21.7 %copy-start.12 = (bf16[2,512,768]{2,1,0:T(8,128)(2,1)S(1)}, bf16[2,512,768]{2,1,0:T(8,128)(2,1)}, u32[]{:S(2)}) copy-start(bf16[2,512,768]{2,1,0:T(8,128)(2,1)} %param.16) | copy-start | bytes 4718596
  7.3 51.5 %all-gather.7.cloned.1.call-start = ((), (), s32[]{:S(2)}) async-start(), calls=%async_computation.12 | async-start | bytes 4423680 | tf_op jit(solution)/shard_map/all_gather | solution.py:405
  11.1 160.9 %all-gather.9.cloned.1.call-start = ((), (), s32[]{:S(2)}) async-start(), calls=%async_computation.13 | async-start | bytes 1327104 | tf_op jit(solution)/shard_map/all_gather | solution.py:408
  11.8 172.4 %all-gather.11.cloned.1.call-start = ((), (), s32[]{:S(2)}) async-start(), calls=%async_computation.14 | async-start | bytes 5308416 | tf_op jit(solution)/shard_map/all_gather | solution.py:409
  64.7 34.9 %all-to-all-start = ((bf16[4,512,640]{2,1,0:T(8,128)(2,1)}), bf16[4,512,640]{2,1,0:T(8,128)(2,1)S(1)}, u32[]{:S(2)}, u32[]{:S(2)}) async-start(bf16[4,512,640]{2,1,0:T(8,128)(2,1)} %shard_map.271), calls=%async_computation | async-start | bytes 5242880 | tf_op jit(solution)/shard_map/all_to_all | solution.py:325
  68.4 128.2 %all-gather.13.cloned.1.call-start = ((), (), s32[]{:S(2)}) async-start(), calls=%async_computation.15 | async-start | bytes 5308416 | tf_op jit(solution)/shard_map/all_gather | solution.py:410
  74.9 29.4 %copy-start.17 = (s32[2]{0:T(128)S(1)}, s32[2]{0:T(128)}, u32[]{:S(2)}) copy-start(s32[2]{0:T(128)} %param.17) | copy-start | bytes 28
  99.6 35.1 %all-to-all-start.2 = ((bf16[4,512,640]{2,1,0:T(8,128)(2,1)}), bf16[4,512,640]{2,1,0:T(8,128)(2,1)}, u32[]{:S(2)}, u32[]{:S(2)}) async-start(bf16[4,512,640]{2,1,0:T(8,128)(2,1)} %shard_map.273), calls=%async_computation.2 | async-start | bytes 5242880 | tf_op jit(solution)/shard_map/all_to_all | solution.py:325
  134.7 28.9 %all-to-all-start.1 = ((bf16[4,512,192]{1,2,0:T(8,128)(2,1)}), bf16[4,512,192]{1,2,0:T(8,128)(2,1)S(1)}, u32[]{:S(2)}, u32[]{:S(2)}) async-start(bf16[4,512,192]{1,2,0:T(8,128)(2,1)} %copy.74), calls=%async_computation.1 | async-start | bytes 1572864 | tf_op jit(solution)/shard_map/all_to_all | solution.py:325
  163.6 14.6 %all-to-all-start.3 = ((bf16[4,512,192]{1,2,0:T(8,128)(2,1)}), bf16[4,512,192]{1,2,0:T(8,128)(2,1)}, u32[]{:S(2)}, u32[]{:S(2)}) async-start(bf16[4,512,192]{1,2,0:T(8,128)(2,1)} %copy.75), calls=%async_computation.3 | async-start | bytes 1572864 | tf_op jit(solution)/shard_map/all_to_all | solution.py:325
  167.9 267.1 %reduce-scatter.15.cloned.1.call-start = ((), (), s32[]{:S(2)}) async-start(), calls=%async_computation.19 | async-start | bytes 1548288
  210.1 14.2 %slice-start = ((s8[4718592]{0:T(1024)(128)(4,1)}), s8[4194304]{0:T(1024)(128)(4,1)S(1)}, s32[]{:S(2)}) async-start(s8[4718592]{0:T(1024)(128)(4,1)} %bitcast.144), calls=%async_computation.20 | async-start | bytes 8388608
  211.2 13.0 %copy-start.10 = (f32[1024,768]{1,0:T(8,128)}, f32[1024,768]{1,0:T(8,128)S(1)}, u32[]{:S(2)}) copy-start(f32[1024,768]{1,0:T(8,128)S(1)} %get-tuple-element.92) | copy-start | bytes 9437188
  211.3 12.9 %copy-start.7 = (f32[1024,768]{1,0:T(8,128)S(1)}, f32[1024,768]{1,0:T(8,128)}, u32[]{:S(2)}) copy-start(f32[1024,768]{1,0:T(8,128)} %copy-done.6) | copy-start | bytes 9437188
  211.3 12.9 %slice-start.1 = ((s8[4718592]{0:T(1024)(128)(4,1)}), s8[524288]{0:T(1024)(128)(4,1)S(1)}, s32[]{:S(2)}) async-start(s8[4718592]{0:T(1024)(128)(4,1)} %bitcast.144), calls=%async_computation.21 | async-start | bytes 1048576
  224.2 6.1 %copy-start.28 = (bf16[1024,3072]{1,0:T(8,128)(2,1)}, bf16[1024,3072]{1,0:T(8,128)(2,1)S(1)}, u32[]{:S(2)}) copy-start(bf16[1024,3072]{1,0:T(8,128)(2,1)S(1)} %get-tuple-element.128) | copy-start | bytes 18874372
  241.3 203.7 %reduce-scatter.9.cloned.1.call-start = ((), (), s32[]{:S(2)}) async-start(), calls=%async_computation.16 | async-start | bytes 5308416 | tf_op jit(solution)/shard_map/reduce_scatter | solution.py:340
  257.7 13.7 %all-to-all-start.4 = ((bf16[4,512,192]{1,2,0:T(8,128)(2,1)}), bf16[4,512,192]{1,2,0:T(8,128)(2,1)S(1)}, u32[]{:S(2)}, u32[]{:S(2)}) async-start(bf16[4,512,192]{1,2,0:T(8,128)(2,1)} %bitcast.126), calls=%async_computation.4 | async-start | bytes 1572864 | tf_op jit(solution)/shard_map/all_to_all | solution.py:325
  261.2 187.4 %reduce-scatter.11.cloned.1.call-start = ((), (), s32[]{:S(2)}) async-start(), calls=%async_computation.17 | async-start | bytes 5308416 | tf_op jit(solution)/shard_map/reduce_scatter | solution.py:340
  272.3 50.0 %all-to-all-start.6 = ((bf16[4,512,192]{1,2,0:T(8,128)(2,1)}), bf16[4,512,192]{1,2,0:T(8,128)(2,1)}, u32[]{:S(2)}, u32[]{:S(2)}) async-start(bf16[4,512,192]{1,2,0:T(8,128)(2,1)} %bitcast.125), calls=%async_computation.6 | async-start | bytes 1572864 | tf_op jit(solution)/shard_map/all_to_all | solution.py:325
  322.3 6.4 %copy-start.1 = (f32[2048,128]{1,0:T(8,128)S(1)}, f32[2048,128]{1,0:T(8,128)}, u32[]{:S(2)}) copy-start(f32[2048,128]{1,0:T(8,128)} %copy-done) | copy-start | bytes 3145732
  322.3 49.3 %all-to-all-start.5 = ((bf16[4,512,640]{2,1,0:T(8,128)(2,1)}), bf16[4,512,640]{2,1,0:T(8,128)(2,1)}, u32[]{:S(2)}, u32[]{:S(2)}) async-start(bf16[4,512,640]{2,1,0:T(8,128)(2,1)} %shard_map.275), calls=%async_computation.5 | async-start | bytes 5242880 | tf_op jit(solution)/shard_map/all_to_all | solution.py:325
  371.6 33.8 %all-to-all-start.7 = ((bf16[4,512,640]{2,1,0:T(8,128)(2,1)}), bf16[4,512,640]{2,1,0:T(8,128)(2,1)S(1)}, u32[]{:S(2)}, u32[]{:S(2)}) async-start(bf16[4,512,640]{2,1,0:T(8,128)(2,1)} %shard_map.277), calls=%async_computation.7 | async-start | bytes 5242880 | tf_op jit(solution)/shard_map/all_to_all | solution.py:325
  375.9 123.8 %reduce-scatter.13.cloned.1.call-start = ((), (), s32[]{:S(2)}) async-start(), calls=%async_computation.18 | async-start | bytes 4202496 | tf_op jit(solution)/shard_map/reduce_scatter | solution.py:340
  436.1 10.7 %collective-permute-start.3 = (bf16[96,896]{0,1:T(8,128)(2,1)S(1)}, bf16[96,896]{0,1:T(8,128)(2,1)}, u32[]{:S(2)}, u32[]{:S(2)}) collective-permute-start(bf16[96,896]{0,1:T(8,128)(2,1)S(1)} %copy.96), channel_id=1, source_target_pairs={{0,8},{8,0},{16,24},{24,16},{1,9},{9,1},{17,25},{25,17},{2,10},{10... | collective-permute-start | bytes 516104 | tf_op jit(solution)/shard_map/ppermute | solution.py:333
  437.5 11.1 %collective-permute-start.4 = (bf16[96,896]{0,1:T(8,128)(2,1)S(1)}, bf16[96,896]{0,1:T(8,128)(2,1)}, u32[]{:S(2)}, u32[]{:S(2)}) collective-permute-start(bf16[96,896]{0,1:T(8,128)(2,1)S(1)} %copy.96), channel_id=1, source_target_pairs={{0,16},{8,24},{16,0},{24,8},{1,17},{9,25},{17,1},{25,9},{2,18},{10... | collective-permute-start | bytes 516104 | tf_op jit(solution)/shard_map/ppermute | solution.py:333
  437.8 13.6 %collective-permute-start.5 = (bf16[96,896]{0,1:T(8,128)(2,1)S(1)}, bf16[96,896]{0,1:T(8,128)(2,1)}, u32[]{:S(2)}, u32[]{:S(2)}) collective-permute-start(bf16[96,896]{0,1:T(8,128)(2,1)S(1)} %copy.96), channel_id=1, source_target_pairs={{0,24},{8,16},{16,8},{24,0},{1,25},{9,17},{17,9},{25,1},{2,26},{10... | collective-permute-start | bytes 516104 | tf_op jit(solution)/shard_map/ppermute | solution.py:333
  445.0 58.1 %copy-start.14 = (bf16[96,3072]{1,0:T(8,128)(2,1)S(1)}, bf16[96,3072]{1,0:T(8,128)(2,1)}, u32[]{:S(2)}) copy-start(bf16[96,3072]{1,0:T(8,128)(2,1)} %reduce-scatter.9.cloned.1.call-done) | copy-start | bytes 1769476
  445.0 54.6 %collective-permute-start.6 = (bf16[96,3072]{1,0:T(8,128)(2,1)}, bf16[96,3072]{1,0:T(8,128)(2,1)}, u32[]{:S(2)}, u32[]{:S(2)}) collective-permute-start(bf16[96,3072]{1,0:T(8,128)(2,1)} %reduce-scatter.9.cloned.1.call-done), channel_id=1, source_target_pairs={{0,8},{8,0},{16,24},{24,16},{1,9},{9,1},{17,25},{25,17},{2,10},{10... | collective-permute-start | bytes 1769480 | tf_op jit(solution)/shard_map/ppermute | solution.py:333
  446.5 53.5 %collective-permute-start.7 = (bf16[96,3072]{1,0:T(8,128)(2,1)}, bf16[96,3072]{1,0:T(8,128)(2,1)}, u32[]{:S(2)}, u32[]{:S(2)}) collective-permute-start(bf16[96,3072]{1,0:T(8,128)(2,1)} %reduce-scatter.9.cloned.1.call-done), channel_id=1, source_target_pairs={{0,16},{8,24},{16,0},{24,8},{1,17},{9,25},{17,1},{25,9},{2,18},{10... | collective-permute-start | bytes 1769480 | tf_op jit(solution)/shard_map/ppermute | solution.py:333
  446.8 54.7 %collective-permute-start.8 = (bf16[96,3072]{1,0:T(8,128)(2,1)}, bf16[96,3072]{1,0:T(8,128)(2,1)}, u32[]{:S(2)}, u32[]{:S(2)}) collective-permute-start(bf16[96,3072]{1,0:T(8,128)(2,1)} %reduce-scatter.9.cloned.1.call-done), channel_id=1, source_target_pairs={{0,24},{8,16},{16,8},{24,0},{1,25},{9,17},{17,9},{25,1},{2,26},{10... | collective-permute-start | bytes 1769480 | tf_op jit(solution)/shard_map/ppermute | solution.py:333
  448.6 6.3 %copy-start.15 = (bf16[384,768]{1,0:T(8,128)(2,1)S(1)}, bf16[384,768]{1,0:T(8,128)(2,1)}, u32[]{:S(2)}) copy-start(bf16[384,768]{1,0:T(8,128)(2,1)} %reduce-scatter.11.cloned.1.call-done) | copy-start | bytes 1769476
  448.6 49.4 %collective-permute-start.10 = (bf16[384,768]{1,0:T(8,128)(2,1)}, bf16[384,768]{1,0:T(8,128)(2,1)}, u32[]{:S(2)}, u32[]{:S(2)}) collective-permute-start(bf16[384,768]{1,0:T(8,128)(2,1)} %reduce-scatter.11.cloned.1.call-done), channel_id=1, source_target_pairs={{0,16},{8,24},{16,0},{24,8},{1,17},{9,25},{17,1},{25,9},{2,18},{10... | collective-permute-start | bytes 1769480 | tf_op jit(solution)/shard_map/ppermute | solution.py:333
  454.9 51.0 %collective-permute-start.11 = (bf16[384,768]{1,0:T(8,128)(2,1)S(1)}, bf16[384,768]{1,0:T(8,128)(2,1)S(1)}, u32[]{:S(2)}, u32[]{:S(2)}) collective-permute-start(bf16[384,768]{1,0:T(8,128)(2,1)S(1)} %copy-done.15), channel_id=1, source_target_pairs={{0,24},{8,16},{16,8},{24,0},{1,25},{9,17},{17,9},{25,1},{2,26},{10... | collective-permute-start | bytes 1769480 | tf_op jit(solution)/shard_map/ppermute | solution.py:333
  498.0 16.3 %collective-permute-start.9 = (bf16[384,768]{1,0:T(8,128)(2,1)S(1)}, bf16[384,768]{1,0:T(8,128)(2,1)S(1)}, u32[]{:S(2)}, u32[]{:S(2)}) collective-permute-start(bf16[384,768]{1,0:T(8,128)(2,1)S(1)} %copy-done.15), channel_id=1, source_target_pairs={{0,8},{8,0},{16,24},{24,16},{1,9},{9,1},{17,25},{25,17},{2,10},{10... | collective-permute-start | bytes 1769480 | tf_op jit(solution)/shard_map/ppermute | solution.py:333
  499.6 16.9 %copy-start.16 = (bf16[96,2432]{1,0:T(8,128)(2,1)S(1)}, bf16[96,2432]{1,0:T(8,128)(2,1)}, u32[]{:S(2)}) copy-start(bf16[96,2432]{1,0:T(8,128)(2,1)} %reduce-scatter.13.cloned.1.call-done) | copy-start | bytes 1400836
  499.6 24.7 %collective-permute-start = (bf16[96,2432]{1,0:T(8,128)(2,1)}, bf16[96,2432]{1,0:T(8,128)(2,1)}, u32[]{:S(2)}, u32[]{:S(2)}) collective-permute-start(bf16[96,2432]{1,0:T(8,128)(2,1)} %reduce-scatter.13.cloned.1.call-done), channel_id=1, source_target_pairs={{0,8},{8,0},{16,24},{24,16},{1,9},{9,1},{17,25},{25,17},{2,10},{10... | collective-permute-start | bytes 1400840 | tf_op jit(solution)/shard_map/ppermute | solution.py:333
  500.0 25.7 %collective-permute-start.1 = (bf16[96,2432]{1,0:T(8,128)(2,1)}, bf16[96,2432]{1,0:T(8,128)(2,1)}, u32[]{:S(2)}, u32[]{:S(2)}) collective-permute-start(bf16[96,2432]{1,0:T(8,128)(2,1)} %reduce-scatter.13.cloned.1.call-done), channel_id=1, source_target_pairs={{0,16},{8,24},{16,0},{24,8},{1,17},{9,25},{17,1},{25,9},{2,18},{10... | collective-permute-start | bytes 1400840 | tf_op jit(solution)/shard_map/ppermute | solution.py:333
  501.4 31.0 %collective-permute-start.2 = (bf16[96,2432]{1,0:T(8,128)(2,1)}, bf16[96,2432]{1,0:T(8,128)(2,1)}, u32[]{:S(2)}, u32[]{:S(2)}) collective-permute-start(bf16[96,2432]{1,0:T(8,128)(2,1)} %reduce-scatter.13.cloned.1.call-done), channel_id=1, source_target_pairs={{0,24},{8,16},{16,8},{24,0},{1,25},{9,17},{17,9},{25,1},{2,26},{10... | collective-permute-start | bytes 1400840 | tf_op jit(solution)/shard_map/ppermute | solution.py:333
  (13 other events, 35.6 us)
Sparse Core Ops, SparseCore 0:
  11.2 47.5 all-gather.6
  60.4 21.4 all-gather.8
  83.5 51.4 all-gather.10
  136.5 50.5 all-gather.12
  241.5 31.4 reduce-scatter.14
  275.2 53.0 reduce-scatter.8
  330.8 53.3 reduce-scatter.10
  427.3 43.2 reduce-scatter.12
